TPU v7x, 256 devices: a whole 4x4x8 slice. The times are simulated.
256 devices in a mesh: dp: 8 (over y, x_lo), expert: 32 (over z, x_hi, core).
Axes of the slice: x: 4 (x_hi: 2, x_lo: 2; x = x_hi * 2 + x_lo), y: 4, z: 8, core: 2. Of those that a mesh axis runs over, the one named last changes fastest.
Arguments:
- tokens: bfloat16 [32768, 2048], P(('dp', 'expert')), may hold values from -6 to 6
- output_gradient: bfloat16 [32768, 2048], P(('dp', 'expert')), may hold values from -6 to 6
- chosen_expert_index: int32 [32768, 6], P(('dp', 'expert')), may hold values from 0 to 31, all different within a row; in each aligned block of 128 rows (0 to 127, 128 to 255, ...) at most 30 rows name the same one
- router_weight: float32 [32768, 6], P(('dp', 'expert')), may hold values from 0.05 to 0.6
- gate_weight: bfloat16 [32, 2048, 704], P('expert'), may hold values from -0.125 to 0.125
- up_weight: bfloat16 [32, 2048, 704], P('expert'), may hold values from -0.125 to 0.125
- down_weight: bfloat16 [32, 704, 2048], P('expert'), may hold values from -0.21875 to 0.21875
- adapter_down_first: float32 [32, 704, 32], P('expert', 'dp'), may hold values from -0.21875 to 0.21875
- adapter_down_second: float32 [32, 32, 2048], P('expert', None, 'dp'), may hold values from -1 to 1
- first_mean_a: float32 [32, 704, 32], P('expert', 'dp'), may hold values from -24 to 24
- squared_mean_a: float32 [32, 704, 32], P('expert', 'dp'), may hold values from 4 to 64
- first_mean_b: float32 [32, 32, 2048], P('expert', None, 'dp'), may hold values from -24 to 24
- squared_mean_b: float32 [32, 32, 2048], P('expert', None, 'dp'), may hold values from 4 to 64
Outputs:
- token_grad: bfloat16 [32768, 2048], P(('dp', 'expert'))
- updated_mean_a: float32 [32, 704, 32], P('expert', 'dp')
- updated_squared_a: float32 [32, 704, 32], P('expert', 'dp')
- adam_delta_first: float32 [32, 704, 32], P('expert', 'dp')
- updated_mean_b: float32 [32, 32, 2048], P('expert', None, 'dp')
- updated_squared_b: float32 [32, 32, 2048], P('expert', None, 'dp')
- adam_delta_second: float32 [32, 32, 2048], P('expert', None, 'dp')
Inputs may be any that keep to these rules, and one draw needn't show every extreme that they name: `chosen_expert_index`: each token names 6 different experts. Among the 128 tokens of one device (aligned blocks of 128 rows) no expert is named more than 30 times, and in every draw some device names some expert exactly 30 times.
All inputs are finite; a program needn't handle non-finite values.
Results may differ from a plain program's by a relative error of at most 0.02.
Values may be sent and summed in bfloat16 or wider, within the bound.
A program may use at most 128 MiB of HBM per device.

v0:
```python
import math

import jax
import jax.numpy as jnp
from jax import lax
from jax.sharding import PartitionSpec as P

adapter_scale = 2.0
beta_one = 0.9
beta_two = 0.999
bias_one = 1.0 - math.exp(1000.0 * math.log(0.9))
bias_two = 1.0 - math.exp(1000.0 * math.log(0.999))
adam_eps = 1e-08
weight_decay = 0.1


def expert_pass(rows_in, row_gradients, gate_mat, up_mat, down_mat, first_adapter, second_adapter):
    contract_trailing = (((1,), (1,)), ((), ()))
    contract_leading = (((0,), (0,)), ((), ()))
    gate_pre = jnp.dot(rows_in, gate_mat, preferred_element_type=jnp.float32)
    up_pre = jnp.dot(rows_in, up_mat, preferred_element_type=jnp.float32)
    sigmoid_gate = jax.nn.sigmoid(gate_pre)
    activated = gate_pre * sigmoid_gate
    expert_activation = (activated * up_pre).astype(jnp.bfloat16)
    narrow_product = jnp.dot(
        expert_activation, first_adapter, preferred_element_type=jnp.float32
    ).astype(jnp.bfloat16)
    narrow_gradient = lax.dot_general(
        row_gradients, second_adapter, contract_trailing, preferred_element_type=jnp.float32
    ).astype(jnp.bfloat16)
    activation_gradient = lax.dot_general(
        row_gradients, down_mat, contract_trailing, preferred_element_type=jnp.float32
    )
    activation_gradient = activation_gradient + adapter_scale * lax.dot_general(
        narrow_gradient, first_adapter, contract_trailing, preferred_element_type=jnp.float32
    )
    gate_grad = (
        activation_gradient * up_pre * sigmoid_gate * (1.0 + gate_pre * (1.0 - sigmoid_gate))
    ).astype(jnp.bfloat16)
    up_grad = (activation_gradient * activated).astype(jnp.bfloat16)
    input_grad = lax.dot_general(
        gate_grad, gate_mat, contract_trailing, preferred_element_type=jnp.float32
    )
    input_grad = (
        input_grad
        + lax.dot_general(up_grad, up_mat, contract_trailing, preferred_element_type=jnp.float32)
    ).astype(jnp.bfloat16)
    first_factor_gradient = adapter_scale * lax.dot_general(
        expert_activation, narrow_gradient, contract_leading, preferred_element_type=jnp.float32
    )
    second_factor_gradient = adapter_scale * lax.dot_general(
        narrow_product, row_gradients, contract_leading, preferred_element_type=jnp.float32
    )
    return (input_grad, first_factor_gradient, second_factor_gradient)


def decoupled_adam_update(param, grad, moment, second):
    moment_new = beta_one * moment + (1.0 - beta_one) * grad
    second_new = beta_two * second + (1.0 - beta_two) * grad * grad
    update = (
        moment_new / bias_one / (jnp.sqrt(second_new / bias_two) + adam_eps) + weight_decay * param
    )
    return (moment_new, second_new, update)


def shards(
    tokens,
    output_gradient,
    chosen_expert_index,
    router_weight,
    gate_weight,
    up_weight,
    down_weight,
    adapter_down_first,
    adapter_down_second,
    first_mean_a,
    squared_mean_a,
    first_mean_b,
    squared_mean_b,
):
    token_count, model_width = tokens.shape
    top_count = chosen_expert_index.shape[1]
    expert_count = lax.axis_size("expert")
    capacity = min(token_count, 5 * token_count * top_count // (4 * expert_count))
    slot_total = expert_count * capacity
    chosen = chosen_expert_index.reshape(-1)
    one_hot = (chosen[:, None] == jnp.arange(expert_count, dtype=jnp.int32)[None, :]).astype(
        jnp.int32
    )
    before = jnp.cumsum(one_hot, axis=0) - one_hot
    rank_in = jnp.sum(before * one_hot, axis=1)
    slot_of = chosen * capacity + rank_in
    per_expert = jnp.sum(one_hot, axis=0).reshape(expert_count, 1)
    source_rows = jnp.arange(token_count * top_count, dtype=jnp.int32) // top_count
    picked = tokens[source_rows]
    scaled = (
        router_weight.reshape(-1)[:, None] * output_gradient[source_rows].astype(jnp.float32)
    ).astype(jnp.bfloat16)
    send_rows = jnp.zeros((slot_total, model_width), jnp.bfloat16).at[slot_of].set(picked)
    send_grads = jnp.zeros((slot_total, model_width), jnp.bfloat16).at[slot_of].set(scaled)
    recv_rows, recv_grads, recv_counts = (
        lax.all_to_all(send_rows, "expert", split_axis=0, concat_axis=0, tiled=True),
        lax.all_to_all(send_grads, "expert", split_axis=0, concat_axis=0, tiled=True),
        lax.all_to_all(per_expert, "expert", split_axis=0, concat_axis=0, tiled=True),
    )
    full_a, full_b = (
        lax.all_gather(adapter_down_first.astype(jnp.bfloat16), "dp", axis=1, tiled=True),
        lax.all_gather(adapter_down_second.astype(jnp.bfloat16), "dp", axis=2, tiled=True),
    )
    gate_mat = gate_weight[0]
    up_mat = up_weight[0]
    down_mat = down_weight[0]
    factor_a = full_a[0]
    factor_b = full_b[0]
    slot_grads, first_factor_gradient, second_factor_gradient = expert_pass(
        recv_rows, recv_grads, gate_mat, up_mat, down_mat, factor_a, factor_b
    )
    returned = lax.all_to_all(slot_grads, "expert", split_axis=0, concat_axis=0, tiled=True)
    gathered = returned[slot_of].astype(jnp.float32).reshape(token_count, top_count, model_width)
    token_grad = jnp.sum(gathered, axis=1).astype(jnp.bfloat16)
    local_first_factor, local_second_factor = (
        lax.psum_scatter(
            first_factor_gradient.astype(jnp.bfloat16), "dp", scatter_dimension=0, tiled=True
        ).astype(jnp.float32),
        lax.psum_scatter(
            second_factor_gradient.astype(jnp.bfloat16), "dp", scatter_dimension=1, tiled=True
        ).astype(jnp.float32),
    )
    updated_mean_a, updated_squared_a, adam_delta_first = decoupled_adam_update(
        adapter_down_first[0], local_first_factor, first_mean_a[0], squared_mean_a[0]
    )
    updated_mean_b, updated_squared_b, adam_delta_second = decoupled_adam_update(
        adapter_down_second[0], local_second_factor, first_mean_b[0], squared_mean_b[0]
    )
    return (
        token_grad,
        updated_mean_a[None],
        updated_squared_a[None],
        adam_delta_first[None],
        updated_mean_b[None],
        updated_squared_b[None],
        adam_delta_second[None],
    )


def solution(mesh):
    placed = (
        P(("dp", "expert"), None),
        P(("dp", "expert"), None),
        P(("dp", "expert"), None),
        P(("dp", "expert"), None),
        P("expert", None, None),
        P("expert", None, None),
        P("expert", None, None),
        P("expert", "dp", None),
        P("expert", None, "dp"),
        P("expert", "dp", None),
        P("expert", "dp", None),
        P("expert", None, "dp"),
        P("expert", None, "dp"),
    )
    return jax.shard_map(
        shards,
        mesh=mesh,
        in_specs=placed,
        out_specs=(
            P(("dp", "expert"), None),
            P("expert", "dp", None),
            P("expert", "dp", None),
            P("expert", "dp", None),
            P("expert", None, "dp"),
            P("expert", None, "dp"),
            P("expert", None, "dp"),
        ),
        check_vma=False,
    )
```

profile of v0, /device:TPU:32, one launch (start us, length us, event | category | flops | bytes accessed | tf_op | source)
XLA Modules:
  0.0 438.0 jit_solution(5627021105662057737)
XLA Ops:
  7.2 0.0 copy-start
  7.2 0.8 broadcast_multiply_fusion
  8.1 0.8 copy.39
  8.8 0.1 eq.29
  9.0 0.1 eq.25
  9.1 0.1 copy.38
  9.2 0.1 mul.142
  9.4 0.8 copy.42
  10.2 0.1 mul.144
  10.3 1.7 reduce-window.6
  12.1 0.3 slice_reduce_fusion
  12.4 0.1 fusion.23
  12.5 32.6 %scatter_custom_fusion = bf16[960,2048]{1,0:T(8,128)(2,1)} fusion(s32[768]{0:T(1024)S(1)} %fusion.38, f32[768]{0:T(1024)S(1)} %mul.144, bf16[]{:T(256)} %constant.16.clone.1, bf16[128,2048]{1,0:T(8,128)(2,1)} %param.14, s32[1024]{0:T(1024)S(1)} %pad_clamp_fusion.1), kind=kCustom, calls=%fused_computation.7 | custom fusion | flops 4718592 | bytes 4464642 | tf_op jit(solution)/shard_map/scatter | solution.py:100
  45.2 5.0 %all_to_all.24 = bf16[32,30,2048]{2,1,0:T(8,128)(2,1)} reshape(bf16[960,2048]{1,0:T(8,128)(2,1)} %scatter_custom_fusion) | data formatting | bytes 7864320 | tf_op jit(solution)/shard_map/all_to_all | solution.py:103
  50.2 11.2 %all-to-all-start = ((bf16[32,30,2048]{2,1,0:T(8,128)(2,1)}), bf16[32,30,2048]{2,1,0:T(8,128)(2,1)}, u32[]{:S(2)}, u32[]{:S(2)}) async-start(bf16[32,30,2048]{2,1,0:T(8,128)(2,1)} %all_to_all.24), calls=%async_computation | async-start | bytes 8388608 | tf_op jit(solution)/shard_map/all_to_all | solution.py:103
  61.5 30.7 %scatter_custom_fusion.1 = bf16[960,2048]{1,0:T(8,128)(2,1)} fusion(s32[768]{0:T(1024)S(1)} %fusion.38, bf16[128,2048]{1,0:T(8,128)(2,1)} %param.13, s32[1024]{0:T(1024)S(1)} %pad_clamp_fusion.1, bf16[]{:T(256)} %constant.16.clone.1), kind=kCustom, calls=%fused_computation.8 | custom fusion | bytes 3932672 | tf_op jit(solution)/shard_map/scatter | solution.py:99
  92.2 5.0 %all_to_all.27 = bf16[32,30,2048]{2,1,0:T(8,128)(2,1)} reshape(bf16[960,2048]{1,0:T(8,128)(2,1)} %scatter_custom_fusion.1) | data formatting | bytes 7864320 | tf_op jit(solution)/shard_map/all_to_all | solution.py:102
  97.2 59.8 %all-to-all-done = bf16[32,30,2048]{2,1,0:T(8,128)(2,1)} async-done(((bf16[32,30,2048]{2,1,0:T(8,128)(2,1)}), bf16[32,30,2048]{2,1,0:T(8,128)(2,1)}, u32[]{:S(2)}, u32[]{:S(2)}) %all-to-all-start) | async-done | bytes 3932192 | tf_op jit(solution)/shard_map/all_to_all | solution.py:103
  157.0 6.1 %all-to-all-start.1 = ((bf16[32,30,2048]{2,1,0:T(8,128)(2,1)}), bf16[32,30,2048]{2,1,0:T(8,128)(2,1)}, u32[]{:S(2)}, u32[]{:S(2)}) async-start(bf16[32,30,2048]{2,1,0:T(8,128)(2,1)} %all_to_all.27), calls=%async_computation.1 | async-start | bytes 8388608 | tf_op jit(solution)/shard_map/all_to_all | solution.py:102
  163.0 0.0 copy-done.5
  163.1 0.0 copy-done.4
  163.1 0.1 copy.43
  163.2 41.7 %all_gather.7 = bf16[1,704,32]{2,0,1:T(2,128)(2,1)S(1)} all-gather(bf16[1,88,32]{2,0,1:T(2,128)(2,1)S(1)} %copy.43), channel_id=1, replica_groups=mesh['dp'=8,'expert'=32] {'dp'}, dimensions={1}, use_global_device_ids=true | all-gather | bytes 50688 | tf_op jit(solution)/shard_map/all_gather | solution.py:107
  204.9 0.1 copy.44
  205.0 44.5 %all_gather.6 = bf16[1,32,2048]{2,1,0:T(8,128)(2,1)S(1)} all-gather(bf16[1,32,256]{2,1,0:T(8,128)(2,1)S(1)} %convert_element_type.56), channel_id=1, replica_groups=mesh['dp'=8,'expert'=32] {'dp'}, dimensions={2}, use_global_device_ids=true | all-gather | bytes 147456 | tf_op jit(solution)/shard_map/all_gather | solution.py:108
  249.5 5.1 %all_to_all.26 = bf16[960,2048]{1,0:T(8,128)(2,1)} reshape(bf16[32,30,2048]{2,1,0:T(8,128)(2,1)} %all-to-all-done) | data formatting | bytes 7864320 | tf_op jit(solution)/shard_map/all_to_all | solution.py:103
  254.6 3.5 convolution_convert_fusion.1
  258.1 0.0 copy-done.1
  258.1 6.6 %fusion.11 = f32[960,704]{0,1:T(8,128)} fusion(bf16[960,2048]{1,0:T(8,128)(2,1)S(1)} %copy-done.1, bf16[1,704,2048]{2,1,0:T(8,128)(2,1)} %param.19), kind=kOutput, calls=%fused_computation.18 | convolution fusion | flops 2768240640 | bytes 9519104 | tf_op jit(solution)/shard_map/dot_general | solution.py:31
  264.7 0.0 all-to-all-done.1
  264.7 5.0 %all_to_all.29 = bf16[960,2048]{1,0:T(8,128)(2,1)} reshape(bf16[32,30,2048]{2,1,0:T(8,128)(2,1)} %all-to-all-done.1) | data formatting | bytes 7864320 | tf_op jit(solution)/shard_map/all_to_all | solution.py:102
  269.7 6.3 %fusion.6 = f32[960,704]{0,1:T(8,128)S(1)} fusion(bf16[960,2048]{1,0:T(8,128)(2,1)} %all_to_all.29, bf16[1,2048,704]{1,2,0:T(8,128)(2,1)} %param.17), kind=kOutput, calls=%fused_computation.13 | convolution fusion | flops 2768240640 | bytes 9519104 | tf_op jit(solution)/shard_map/dot_general | solution.py:20
  276.0 0.0 copy-done
  276.0 0.0 copy-done.2
  276.0 0.0 copy-start.3
  276.0 4.6 %multiply_convert_fusion.2 = (bf16[960,704]{0,1:T(8,128)(2,1)}, f32[960,704]{0,1:T(8,128)S(1)}) fusion(f32[960,704]{0,1:T(8,128)S(1)} %fusion.6, bf16[960,2048]{1,0:T(8,128)(2,1)S(1)} %copy-done.2, bf16[1,2048,704]{1,2,0:T(8,128)(2,1)S(1)} %copy-done), kind=kOutput, calls=%fused_computation.20 | convolution fusion | flops 2772295680 | bytes 13574144 | tf_op jit(solution)/shard_map/dot_general | solution.py:21
  280.6 0.0 copy-done.3
  280.6 0.6 multiply_add_fusion
  281.2 1.2 copy-done.10
  282.4 3.9 fusion.4
  286.4 4.9 %add_convert_fusion = bf16[960,2048]{1,0:T(8,128)(2,1)} fusion(f32[960,2048]{1,0:T(8,128)S(1)} %fusion.4, bf16[1,2048,704]{1,2,0:T(8,128)(2,1)S(1)} %copy-done, f32[960,704]{0,1:T(8,128)S(1)} %multiply_add_fusion, f32[960,704]{0,1:T(8,128)S(1)} %fusion.6), kind=kOutput, calls=%fused_computation.5 | convolution fusion | flops 2776227840 | bytes 20086784 | tf_op jit(solution)/shard_map/dot_general | solution.py:46
  291.3 5.0 %all_to_all.30 = bf16[32,30,2048]{2,1,0:T(8,128)(2,1)} reshape(bf16[960,2048]{1,0:T(8,128)(2,1)} %add_convert_fusion) | data formatting | bytes 7864320 | tf_op jit(solution)/shard_map/all_to_all | solution.py:118
  296.3 12.6 %all-to-all-start.2 = ((bf16[32,30,2048]{2,1,0:T(8,128)(2,1)}), bf16[32,30,2048]{2,1,0:T(8,128)(2,1)}, u32[]{:S(2)}, u32[]{:S(2)}) async-start(bf16[32,30,2048]{2,1,0:T(8,128)(2,1)} %all_to_all.30), calls=%async_computation.2 | async-start | bytes 8388608 | tf_op jit(solution)/shard_map/all_to_all | solution.py:118
  309.0 0.0 reduce-scatter.3.cloned.1.call-start
  309.0 0.0 copy-done.11
  309.0 0.6 dynamic-slice
  310.3 0.0 copy-start.8
  310.3 0.0 copy-start.9
  310.3 0.0 copy-start.6
  310.3 0.0 copy-start.7
  310.3 4.3 fusion.14
  314.6 0.0 reduce-scatter.3.cloned.1.call-update
  314.6 1.9 fusion.18
  316.5 34.1 %all-reduce = bf16[704,32]{0,1:T(8,128)(2,1)S(1)} all-reduce(bf16[704,32]{0,1:T(8,128)(2,1)S(1)} %fusion.18), channel_id=2, replica_groups=mesh['dp'=8,'expert'=32] {'dp'}, use_global_device_ids=true, to_apply=%region_6.7.clone | all-reduce | flops 22528 | bytes 90112
  350.7 0.0 copy-done.8
  350.7 0.0 copy-done.9
  350.7 0.7 fusion.35
  351.4 3.1 reduce-scatter.3.cloned.1.call-done
  354.5 1.4 fusion.30
  355.8 48.5 %all-to-all-done.2 = bf16[32,30,2048]{2,1,0:T(8,128)(2,1)} async-done(((bf16[32,30,2048]{2,1,0:T(8,128)(2,1)}), bf16[32,30,2048]{2,1,0:T(8,128)(2,1)}, u32[]{:S(2)}, u32[]{:S(2)}) %all-to-all-start.2) | async-done | bytes 3932192 | tf_op jit(solution)/shard_map/all_to_all | solution.py:118
  404.3 5.0 %all_to_all.32 = bf16[960,2048]{1,0:T(8,128)(2,1)} reshape(bf16[32,30,2048]{2,1,0:T(8,128)(2,1)} %all-to-all-done.2) | data formatting | bytes 7864320 | tf_op jit(solution)/shard_map/all_to_all | solution.py:118
  409.3 9.7 %gather_fusion = bf16[768,2048]{1,0:T(8,128)(2,1)} fusion(bf16[960,2048]{1,0:T(8,128)(2,1)} %all_to_all.32, s32[1024]{0:T(1024)S(1)} %pad_clamp_fusion), kind=kCustom, calls=%fused_computation.2 | custom fusion | bytes 6294528 | tf_op jit(solution)/shard_map/gather | solution.py:119
  419.0 6.3 %gather.14 = bf16[128,6,2048]{2,1,0:T(8,128)(2,1)} reshape(bf16[768,2048]{1,0:T(8,128)(2,1)} %gather_fusion) | data formatting | bytes 6291456 | tf_op jit(solution)/shard_map/gather | solution.py:119
  425.2 5.7 %reduce_sum.25 = bf16[128,2048]{1,0:T(8,128)(2,1)} reduce(bf16[128,6,2048]{2,1,0:T(8,128)(2,1)} %gather.14, bf16[]{:T(256)} %constant.16.clone.1), dimensions={1}, to_apply=%region_5.6 | reduce | flops 1310720 | bytes 3670018 | tf_op jit(solution)/shard_map/reduce_sum | solution.py:120
  (16 shorter events, 0.1 us)
Async XLA Ops:
  7.2 268.8 %copy-start = (bf16[1,2048,704]{1,2,0:T(8,128)(2,1)S(1)}, bf16[1,2048,704]{1,2,0:T(8,128)(2,1)}, u32[]{:S(2)}) copy-start(bf16[1,2048,704]{1,2,0:T(8,128)(2,1)} %param.18) | copy-start | bytes 8650756
  50.2 106.8 %all-to-all-start = ((bf16[32,30,2048]{2,1,0:T(8,128)(2,1)}), bf16[32,30,2048]{2,1,0:T(8,128)(2,1)}, u32[]{:S(2)}, u32[]{:S(2)}) async-start(bf16[32,30,2048]{2,1,0:T(8,128)(2,1)} %all_to_all.24), calls=%async_computation | async-start | bytes 8388608 | tf_op jit(solution)/shard_map/all_to_all | solution.py:103
  97.2 65.9 %copy-start.5 = (f32[1,88,32]{1,2,0:T(8,128)S(1)}, f32[1,88,32]{1,2,0:T(8,128)}, u32[]{:S(2)}) copy-start(f32[1,88,32]{1,2,0:T(8,128)} %param.20) | copy-start | bytes 33796
  97.2 65.9 %copy-start.4 = (f32[1,32,256]{2,1,0:T(8,128)S(1)}, f32[1,32,256]{2,1,0:T(8,128)}, u32[]{:S(2)}) copy-start(f32[1,32,256]{2,1,0:T(8,128)} %param.21) | copy-start | bytes 98308
  157.0 107.7 %all-to-all-start.1 = ((bf16[32,30,2048]{2,1,0:T(8,128)(2,1)}), bf16[32,30,2048]{2,1,0:T(8,128)(2,1)}, u32[]{:S(2)}, u32[]{:S(2)}) async-start(bf16[32,30,2048]{2,1,0:T(8,128)(2,1)} %all_to_all.27), calls=%async_computation.1 | async-start | bytes 8388608 | tf_op jit(solution)/shard_map/all_to_all | solution.py:102
  254.6 3.5 copy-start.1
  269.7 6.3 %copy-start.2 = (bf16[960,2048]{1,0:T(8,128)(2,1)S(1)}, bf16[960,2048]{1,0:T(8,128)(2,1)}, u32[]{:S(2)}) copy-start(bf16[960,2048]{1,0:T(8,128)(2,1)} %all_to_all.29) | copy-start | bytes 11796484
  276.0 4.6 %copy-start.3 = (f32[960,704]{0,1:T(8,128)S(1)}, f32[960,704]{0,1:T(8,128)}, u32[]{:S(2)}) copy-start(f32[960,704]{0,1:T(8,128)} %fusion.11) | copy-start | bytes 8110084
  280.6 1.8 copy-start.10
  296.3 12.7 %copy-start.11 = (u32[256]{0:T(256)S(1)}, u32[256]{0:T(256)}, u32[]{:S(2)}) copy-start(u32[256]{0:T(256)} %constant.70) | copy-start | bytes 3076
  296.3 108.0 %all-to-all-start.2 = ((bf16[32,30,2048]{2,1,0:T(8,128)(2,1)}), bf16[32,30,2048]{2,1,0:T(8,128)(2,1)}, u32[]{:S(2)}, u32[]{:S(2)}) async-start(bf16[32,30,2048]{2,1,0:T(8,128)(2,1)} %all_to_all.30), calls=%async_computation.2 | async-start | bytes 8388608 | tf_op jit(solution)/shard_map/all_to_all | solution.py:118
  309.0 45.5 %reduce-scatter.3.cloned.1.call-start = ((), (), s32[]{:S(2)}) async-start(), calls=%async_computation.4 | async-start | bytes 147456 | tf_op jit(solution)/shard_map/reduce_scatter | solution.py:125
  310.3 40.4 %copy-start.8 = (f32[1,88,32]{1,2,0:T(8,128)S(1)}, f32[1,88,32]{1,2,0:T(8,128)}, u32[]{:S(2)}) copy-start(f32[1,88,32]{1,2,0:T(8,128)} %param.22) | copy-start | bytes 33796
  310.3 40.4 %copy-start.9 = (f32[1,88,32]{1,2,0:T(8,128)S(1)}, f32[1,88,32]{1,2,0:T(8,128)}, u32[]{:S(2)}) copy-start(f32[1,88,32]{1,2,0:T(8,128)} %param.23) | copy-start | bytes 33796
  310.3 44.1 %copy-start.6 = (f32[1,32,256]{2,1,0:T(8,128)S(1)}, f32[1,32,256]{2,1,0:T(8,128)}, u32[]{:S(2)}) copy-start(f32[1,32,256]{2,1,0:T(8,128)} %param.24) | copy-start | bytes 98308
  310.3 44.1 %copy-start.7 = (f32[1,32,256]{2,1,0:T(8,128)S(1)}, f32[1,32,256]{2,1,0:T(8,128)}, u32[]{:S(2)}) copy-start(f32[1,32,256]{2,1,0:T(8,128)} %param.25) | copy-start | bytes 98308
Sparse Core Ops, SparseCore 0:
  314.8 39.6 reduce-scatter.2
where the time goes:
time: 443 us; the launch traced here: 438 us
  blocking collectives  120 us (27%)
  waiting for transfers between devices  111 us (25%)
  local copies, waits for them, and re-layouts  81.4 us (18%)
  other arithmetic  43.2 us (10%)
  matrix products  36.5 us (8%)
  starting transfers between devices  30 us (7%)
  between operations  15.2 us (3%)
    all_to_all x1, waiting for transfers between devices, shards(): lax.all_to_all(send_grads, 'expert', split_axis=0, concat_axis=0, tiled=T...  59.8 us
    all_to_all x1, waiting for transfers between devices, shards(): lax.all_to_all(slot_grads, 'expert', split_axis=0, concat_axis=0, tiled=T...  48.5 us
    all_gather x1, blocking collectives, shards(): lax.all_gather(adapter_down_second.astype(jnp.bfloat16), 'dp', axis=2, ti...  44.5 us
    all_gather x1, blocking collectives, shards(): lax.all_gather(adapter_down_first.astype(jnp.bfloat16), 'dp', axis=1, til...  41.7 us
    unnamed x1, blocking collectives  34.1 us
    scatter x1, other arithmetic, shards(): jnp.zeros((slot_total, model_width), jnp.bfloat16).at[slot_of].set(scaled)  32.6 us
    scatter x1, local copies, waits for them, and re-layouts, shards(): jnp.zeros((slot_total, model_width), jnp.bfloat16).at[slot_of].set(picked)  30.7 us
    gather x2, local copies, waits for them, and re-layouts, shards(): returned[slot_of].astype(jnp.float32)  16 us
  transfers between devices with their start and end apart: 4, of which 3 were waited for; matrix products, arithmetic and copies ran while one was open for 11% of the time, Pallas kernels for 0%

commit v1 on v0

v1 whole, which is shorter than its diff:
```python
import functools
import math

import jax
import jax.numpy as jnp
from jax import lax
from jax.experimental import pallas as pl
from jax.experimental.pallas import tpu as pltpu
from jax.sharding import PartitionSpec as P

adapter_scale = 2.0
beta_one = 0.9
beta_two = 0.999
bias_one = 1.0 - math.exp(1000.0 * math.log(0.9))
bias_two = 1.0 - math.exp(1000.0 * math.log(0.999))
adam_eps = 1e-08
weight_decay = 0.1

MESH = pl.DeviceIdType.MESH
NT = (((1,), (1,)), ((), ()))
NN = (((1,), (0,)), ((), ()))
TN = (((0,), (0,)), ((), ()))
RING = 8
SLOT = 32
RANK = 32
PART = 384
f32 = jnp.float32
bf16 = jnp.bfloat16


def dot(a, b, dims=NN):
    return lax.dot_general(a, b, dims, preferred_element_type=f32)


def kernel(
    tok_ref, grad_ref, chosen_ref, weight_ref, gate_ref, up_ref, down_ref, shard_ref,
    out_ref, sum_ref,
    tg, wg, wu, wd, ab, gs, gr, ms, mr, rp, rm, factor,
    ag_send, ag_recv, w_send, w_recv, rs_send, rs_recv, ab_send, ab_recv,
    gab_send, gab_recv, m_send, m_recv, own_sem,
):
    tokens, width = tok_ref.shape
    units = gate_ref.shape[2]
    half = width // 2
    dp = lax.axis_index("dp")
    ex = lax.axis_index("expert")
    z, xh, core = ex // 4, (ex // 2) % 2, ex % 2
    y, xl = dp // 2, dp % 2

    def at(zz, hh, cc):
        return (zz * 2 + hh) * 2 + cc

    zp = (dp, at((z + 1) % RING, xh, core))
    zm = (dp, at((z + RING - 1) % RING, xh, core))
    sib = (dp, at(z, xh, 1 - core))
    cross = (y * 2 + 1 - xl, at(z, 1 - xh, core))
    xlo = (y * 2 + 1 - xl, ex)
    yp = (((y + 1) % 4) * 2 + xl, ex)
    ym = (((y + 3) % 4) * 2 + xl, ex)

    def plane(k, j):
        hh = xh if k < 2 else 1 - xh
        cc = core if k % 2 == 0 else 1 - core
        return ((dp + j) % 8, at(z, hh, cc))

    def each_peer(f):
        for k in range(4):
            lax.fori_loop(1 if k == 0 else 0, 8, functools.partial(lambda k, j, c: (f(k, j), c)[1], k), 0)

    barrier = pltpu.get_barrier_semaphore()

    def greet(device):
        pl.semaphore_signal(barrier, inc=1, device_id=device, device_id_type=MESH)

    each_peer(lambda k, j: greet(plane(k, j)))
    lax.fori_loop(1, RING, lambda r, c: (greet((dp, at((z + r) % RING, xh, core))), c)[1], 0)
    pl.semaphore_wait(barrier, 31 + RING - 1)

    def remote(src, dst, send, recv, device):
        return pltpu.make_async_remote_copy(
            src_ref=src, dst_ref=dst, send_sem=send, recv_sem=recv, device_id=device, device_id_type=MESH
        )

    def piece(ref, h):
        return ref.at[:, pl.ds(h * half, half)]

    def ag(a, way, hop, h):
        own = tok_ref if a == 0 else grad_ref
        here = hop if way == 0 else (RING - hop) % RING
        there = hop + 1 if way == 0 else RING - hop - 1
        src = own if hop == 0 else tg.at[a, here]
        return remote(
            piece(src, h), piece(tg.at[a, there], h), ag_send.at[a, way, hop, h],
            ag_recv.at[a, there, h], zp if way == 0 else zm,
        )

    def ag_has(hop, way, h):
        return hop < 3 or h == way

    for a in range(2):
        for h in range(2):
            for way in range(2):
                ag(a, way, 0, h).start()
    own_tok = pltpu.make_async_copy(tok_ref, tg.at[0, 0], own_sem.at[0])
    own_grad = pltpu.make_async_copy(grad_ref, tg.at[1, 0], own_sem.at[1])
    own_tok.start()
    own_grad.start()

    own_w = (gate_ref.at[0], up_ref.at[0], down_ref.at[0])
    all_w = (wg, wu, wd)

    def part(ref, m, q, n):
        size = width // 8 * n
        begin = pl.ds(pl.multiple_of(q * (width // 8), width // 8), size)
        return ref.at[begin, :] if m < 2 else ref.at[:, begin]

    c_piece = y * 2 + 1 - xl
    s_piece = y * 2 + xl

    def piece_of(row, name):
        return (row % 4) * 2 + (1 - xl if name == 0 else xl)

    def w_copy(m, n):
        src2 = all_w[m].at[2]
        if n == 0:
            return remote(own_w[m], all_w[m].at[1], w_send.at[m, 0], w_recv.at[m, 0], sib)
        if n == 1:
            return remote(part(own_w[m], m, dp, 1), part(src2, m, dp, 1), w_send.at[m, 1], w_recv.at[m, 1], cross)
        if n == 2:
            return remote(part(src2, m, c_piece, 1), part(src2, m, c_piece, 1), w_send.at[m, 2], w_recv.at[m, 2], xlo)
        if n < 9:
            q = {
                3: piece_of(y, 0), 4: piece_of(y, 1), 5: piece_of(y, 0), 6: piece_of(y, 1),
                7: piece_of(y + 3, 0), 8: piece_of(y + 1, 1),
            }[n]
            device = yp if n in (3, 4, 7) else ym
            return remote(part(src2, m, q, 1), part(src2, m, q, 1), w_send.at[m, n], w_recv.at[m, n], device)
        row = (y + (0, 3, 1, 2)[n - 9]) % 4
        return remote(
            part(src2, m, row * 2, 2), part(all_w[m].at[3], m, row * 2, 2), w_send.at[m, n], w_recv.at[m, n], sib
        )

    own_copies = [pltpu.make_async_copy(own_w[m], all_w[m].at[0], own_sem.at[2 + m]) for m in range(3)]
    for m in range(3):
        w_copy(m, 1).start()
    for m in range(3):
        w_copy(m, 0).start()
        own_copies[m].start()

    ab[pl.ds(dp, 1)] = shard_ref[...][None]

    def ab_copy(k, j):
        return remote(shard_ref, ab.at[k * 8 + dp], ab_send, ab_recv, plane(k, j))

    each_peer(lambda k, j: ab_copy(k, j).start())

    ids = lax.broadcasted_iota(jnp.int32, (4 * RING, tokens), 0)
    named = jnp.zeros((4 * RING, tokens), f32)
    weighted = jnp.zeros((4 * RING, tokens), f32)
    for k in range(chosen_ref.shape[0]):
        hit = ids == chosen_ref[k : k + 1, :]
        named = jnp.where(hit, 1.0, named)
        weighted = jnp.where(hit, weight_ref[k : k + 1, :], weighted)
    earlier = lax.broadcasted_iota(jnp.int32, (tokens, tokens), 0) < lax.broadcasted_iota(
        jnp.int32, (tokens, tokens), 1
    )
    rank = dot(named.astype(bf16), jnp.where(earlier, 1.0, 0.0).astype(bf16))
    rank = jnp.where(named > 0.5, rank, -1.0)
    for zz in range(RING):
        ms[zz, 0:4, :] = rank[zz * 4 : zz * 4 + 4]
        ms[zz, 4:8, :] = weighted[zz * 4 : zz * 4 + 4]
    mr[pl.ds(0, 1)] = ms[pl.ds(z, 1)]

    def m_copy(r):
        there = (z + r) % RING
        return remote(ms.at[there], mr.at[r], m_send, m_recv, (dp, at(there, xh, core)))

    lax.fori_loop(1, RING, lambda r, c: (m_copy(r).start(), c)[1], 0)

    def ag_arrive(a, hop):
        for h in range(2):
            for way in range(2):
                if not ag_has(hop - 1, way, h):
                    continue
                ag(a, way, hop - 1, h).wait_recv()
                if hop < 4 and ag_has(hop, way, h):
                    ag(a, way, hop, h).start()

    for m in range(3):
        w_copy(m, 1).wait_recv()
        for n in (2, 3, 5):
            w_copy(m, n).start()
    ag_arrive(0, 1)
    for m in range(3):
        w_copy(m, 2).wait_recv()
        for n in (4, 6, 9):
            w_copy(m, n).start()
    ag_arrive(1, 1)
    ag_arrive(0, 2)
    ag_arrive(1, 2)
    for m in range(3):
        w_copy(m, 3).wait_recv()
        w_copy(m, 7).start()
        w_copy(m, 6).wait_recv()
        w_copy(m, 8).start()
    ag_arrive(0, 3)
    for m in range(3):
        w_copy(m, 4).wait_recv()
        w_copy(m, 10).start()
        w_copy(m, 5).wait_recv()
        w_copy(m, 11).start()
    ag_arrive(1, 3)
    for m in range(3):
        w_copy(m, 7).wait_recv()
        w_copy(m, 8).wait_recv()
        w_copy(m, 12).start()
    ag_arrive(0, 4)
    ag_arrive(1, 4)
    own_tok.wait()
    own_grad.wait()
    for c in own_copies:
        c.wait()
    for m in range(3):
        for n in (0, 9, 10, 11, 12):
            w_copy(m, n).wait_recv()
    for m in range(3):
        for n in range(13):
            w_copy(m, n).wait_send()
    for a in range(2):
        for hop in range(4):
            for h in range(2):
                for way in range(2):
                    if ag_has(hop, way, h):
                        ag(a, way, hop, h).wait_send()
    many = ab.at[pl.ds(0, 31)]
    pltpu.make_async_copy(many, many, ab_recv).wait()
    pltpu.make_async_copy(many, many, ab_send).wait()
    seven = mr.at[pl.ds(1, RING - 1)]
    pltpu.make_async_copy(seven, seven, m_recv).wait()
    pltpu.make_async_copy(seven, seven, m_send).wait()

    slots = lax.broadcasted_iota(jnp.int32, (SLOT, tokens), 0).astype(f32)

    def row_of(k):
        hh = xh if k < 2 else 1 - xh
        cc = core if k % 2 == 0 else 1 - core
        return hh * 2 + cc

    def picks(b):
        return [
            jnp.where(slots == mr[b, pl.ds(row_of(k), 1), :], 1.0, 0.0) for k in range(4)
        ]

    def gather(b, carry):
        chosen = picks(b)
        scale = jnp.concatenate(
            [
                jnp.sum(chosen[k] * mr[b, pl.ds(row_of(k) + 4, 1), :], axis=1, keepdims=True)
                for k in range(4)
            ],
            axis=0,
        )
        pick = jnp.concatenate(chosen, axis=0).astype(bf16)
        tg[0, b] = dot(pick, tg[0, b]).astype(bf16)
        tg[1, b] = (dot(pick, tg[1, b]) * scale).astype(bf16)
        return carry

    lax.fori_loop(0, RING, gather, 0)

    unit_count = units // 8

    def spread(d):
        i = lax.broadcasted_iota(jnp.int32, (128, units), 0)
        j = lax.broadcasted_iota(jnp.int32, (128, units), 1)
        return jnp.where((j - d * unit_count == i) & (i < unit_count), 1.0, 0.0).astype(bf16)

    def assemble(k, carry):
        def one(d, total):
            return total + dot(ab[k * 8 + d, :, 0:128], spread(d))

        factor[k] = lax.fori_loop(0, 8, one, jnp.zeros((RANK, units), f32)).astype(bf16)
        return carry

    lax.fori_loop(0, 4, assemble, 0)

    def expert(k, carry):
        where = pl.ds(pl.multiple_of(k * SLOT, SLOT), SLOT)
        rows = RING * SLOT
        x = tg[0, :, where, :].reshape(rows, width)
        g = tg[1, :, where, :].reshape(rows, width)
        a_t = factor[k]
        b_all = jnp.concatenate([ab[k * 8 + d, :, 128:PART] for d in range(8)], axis=1)
        gate_pre = dot(x, wg[k])
        up_pre = dot(x, wu[k])
        s = jax.nn.sigmoid(gate_pre)
        activated = gate_pre * s
        hidden = (activated * up_pre).astype(bf16)
        low_rank = dot(hidden, a_t, NT).astype(bf16)
        low_grad = dot(g, b_all, NT).astype(bf16)
        hidden_grad = dot(g, wd[k], NT) + adapter_scale * dot(low_grad, a_t)
        gate_grad = (hidden_grad * up_pre * s * (1.0 + gate_pre * (1.0 - s))).astype(bf16)
        up_grad = (hidden_grad * activated).astype(bf16)
        pair = dot(gate_grad, wg[k], NT) + dot(up_grad, wu[k], NT)
        tg[0, :, where, :] = pair.astype(bf16).reshape(RING, SLOT, width)
        grad_a = (adapter_scale * dot(low_grad, hidden, TN)).astype(bf16)
        grad_b = (adapter_scale * dot(low_rank, g, TN)).astype(bf16)
        for d in range(8):
            gs[k * 8 + d, :, 0:128] = dot(grad_a, spread(d), NT).astype(bf16)
            gs[k * 8 + d, :, 128:PART] = grad_b[:, d * 256 : d * 256 + 256]
        return carry

    lax.fori_loop(0, 4, expert, 0)

    def gab_copy(k, j):
        return remote(gs.at[k * 8 + (dp + j) % 8], gr.at[k * 8 + dp], gab_send, gab_recv, plane(k, j))

    each_peer(lambda k, j: gab_copy(k, j).start())

    def combine(b, carry):
        pick = jnp.concatenate(picks(b), axis=0).astype(bf16)
        tg[0, b] = dot(pick, tg[0, b], TN).astype(bf16)
        return carry

    lax.fori_loop(0, RING, combine, 0)

    def rs(way, step, h):
        here = 4 + step if way == 0 else 4 - step
        landing = rp if way == 0 else rm
        return remote(
            piece(tg.at[0, here], h), landing.at[step, h], rs_send.at[way, step, h],
            rs_recv.at[way, step, h], zp if way == 0 else zm,
        )

    def rs_add(way, step, h):
        rs(way, step, h).wait_recv()
        landing = rp if way == 0 else rm
        here = 5 + step if way == 0 else 3 - step
        cols = slice(h * half, h * half + half)
        tg[0, here, :, cols] = (tg[0, here, :, cols].astype(f32) + landing[step, h].astype(f32)).astype(bf16)
        rs(way, step + 1, h).start()

    for way in range(2):
        rs(way, 0, way).start()
        rs(way, 1, 1 - way).start()
    for step in range(3):
        for way in range(2):
            if step > 0:
                rs_add(way, step, 1 - way)
        for way in range(2):
            rs_add(way, step, way)
    for h in range(2):
        rs(0, 3, h).wait_recv()
        rs(1, 3, h).wait_recv()
        cols = slice(h * half, h * half + half)
        out_ref[:, cols] = (
            tg[0, 0, :, cols].astype(f32) + rp[3, h].astype(f32) + rm[3, h].astype(f32)
        ).astype(bf16)

    many_g = gr.at[pl.ds(0, 31)]
    pltpu.make_async_copy(many_g, many_g, gab_recv).wait()
    pltpu.make_async_copy(many_g, many_g, gab_send).wait()
    gr[pl.ds(dp, 1)] = gs[pl.ds(dp, 1)]
    sum_ref[...] = lax.fori_loop(
        0, 32, lambda i, total: total + gr[i].astype(f32), jnp.zeros((RANK, PART), f32)
    )
    for way in range(2):
        for step in range(4):
            for h in range(2):
                if step > 0 or h == way:
                    rs(way, step, h).wait_send()


def expert_layer(tokens, grads, chosen, weights, gate, up, down, shard):
    count, width = tokens.shape
    units = gate.shape[2]
    vmem = pl.BlockSpec(memory_space=pltpu.VMEM)
    hbm = pl.BlockSpec(memory_space=pl.ANY)
    dma = pltpu.SemaphoreType.DMA
    return pl.pallas_call(
        kernel,
        out_shape=(
            jax.ShapeDtypeStruct((count, width), bf16),
            jax.ShapeDtypeStruct((RANK, PART), f32),
        ),
        in_specs=[hbm, hbm, vmem, vmem, hbm, hbm, hbm, vmem],
        out_specs=(vmem, vmem),
        scratch_shapes=[
            pltpu.VMEM((2, RING, count, width), bf16),
            pltpu.VMEM((4, width, units), bf16),
            pltpu.VMEM((4, width, units), bf16),
            pltpu.VMEM((4, units, width), bf16),
            pltpu.VMEM((32, RANK, PART), bf16),
            pltpu.VMEM((32, RANK, PART), bf16),
            pltpu.VMEM((32, RANK, PART), bf16),
            pltpu.VMEM((RING, 8, count), f32),
            pltpu.VMEM((RING, 8, count), f32),
            pltpu.VMEM((4, 2, count, width // 2), bf16),
            pltpu.VMEM((4, 2, count, width // 2), bf16),
            pltpu.VMEM((4, RANK, units), bf16),
            dma((2, 2, 4, 2)),
            dma((2, 8, 2)),
            dma((3, 13)),
            dma((3, 13)),
            dma((2, 4, 2)),
            dma((2, 4, 2)),
            dma,
            dma,
            dma,
            dma,
            dma,
            dma,
            dma((5,)),
        ],
        compiler_params=pltpu.CompilerParams(
            collective_id=0, has_side_effects=True, vmem_limit_bytes=60 * 1024 * 1024
        ),
        name="expert_layer",
    )(tokens, grads, chosen, weights, gate, up, down, shard)


def decoupled_adam_update(param, grad, moment, second):
    moment_new = beta_one * moment + (1.0 - beta_one) * grad
    second_new = beta_two * second + (1.0 - beta_two) * grad * grad
    update = (
        moment_new / bias_one / (jnp.sqrt(second_new / bias_two) + adam_eps) + weight_decay * param
    )
    return (moment_new, second_new, update)


def shards(
    tokens,
    output_gradient,
    chosen_expert_index,
    router_weight,
    gate_weight,
    up_weight,
    down_weight,
    adapter_down_first,
    adapter_down_second,
    first_mean_a,
    squared_mean_a,
    first_mean_b,
    squared_mean_b,
):
    unit_count = adapter_down_first.shape[1]
    shard = jnp.concatenate(
        [
            jnp.pad(adapter_down_first[0].T, ((0, 0), (0, 128 - unit_count))),
            adapter_down_second[0],
        ],
        axis=1,
    ).astype(bf16)
    token_grad, sums = expert_layer(
        tokens,
        output_gradient,
        chosen_expert_index.T,
        router_weight.T,
        gate_weight,
        up_weight,
        down_weight,
        shard,
    )
    updated_a = decoupled_adam_update(
        adapter_down_first[0], sums[:, :unit_count].T, first_mean_a[0], squared_mean_a[0]
    )
    updated_b = decoupled_adam_update(
        adapter_down_second[0], sums[:, 128:], first_mean_b[0], squared_mean_b[0]
    )
    return (token_grad, *(v[None] for v in updated_a), *(v[None] for v in updated_b))


def solution(mesh):
    rows = P(("dp", "expert"), None)
    frozen = P("expert", None, None)
    first = P("expert", "dp", None)
    second = P("expert", None, "dp")
    return jax.shard_map(
        shards,
        mesh=mesh,
        in_specs=(rows,) * 4 + (frozen,) * 3 + (first, second, first, first, second, second),
        out_specs=(rows, first, first, first, second, second, second),
        check_vma=False,
    )
```

time: 443 us -> 202 us (0.46)
  Pallas kernels: 0 us -> 184 us
  blocking collectives: 120 us -> 0 us
  waiting for transfers between devices: 111 us -> 0 us
  local copies, waits for them, and re-layouts: 81.4 us -> 9.42 us
  other arithmetic: 43.2 us -> 4.86 us
  matrix products: 36.5 us -> 0 us
  starting transfers between devices: 30 us -> 0 us
  between operations: 15.2 us -> 0.69 us
    pallas_call x0 -> x1, Pallas kernels: none -> 184 us  [expert_layer(): pl.pallas_call(kernel, out_shape=(jax.ShapeDtypeStruct((count, width), bf...]
    all_to_all x3 -> x0, waiting for transfers between devices: 108 us -> none  [the longest x1 59.8 us: shards(): lax.all_to_all(send_grads, 'expert', split_axis=0, concat_axis=0, tiled=T...]
    all_gather x2 -> x0, blocking collectives: 86.2 us -> none  [the longest x1 44.5 us: shards(): lax.all_gather(adapter_down_second.astype(jnp.bfloat16), 'dp', axis=2, ti...]
    dot_general x9 -> x0, matrix products: 36.5 us -> none  [the longest x1 6.58 us: expert_pass(): lax.dot_general(row_gradients, down_mat, contract_trailing, preferred_ele...]
    unnamed x1 -> x0, blocking collectives: 34.1 us -> none
    scatter x1 -> x0, other arithmetic: 32.6 us -> none  [shards(): jnp.zeros((slot_total, model_width), jnp.bfloat16).at[slot_of].set(scaled)]
    scatter x1 -> x0, local copies, waits for them, and re-layouts: 30.7 us -> none  [shards(): jnp.zeros((slot_total, model_width), jnp.bfloat16).at[slot_of].set(picked)]
    all_to_all x6 -> x0, local copies, waits for them, and re-layouts: 30.2 us -> none  [the longest x2 10.1 us: shards(): lax.all_to_all(send_grads, 'expert', split_axis=0, concat_axis=0, tiled=T...]
  transfers between devices with their start and end apart: 4 -> 0, of which waited for: 3 -> 0; matrix products, arithmetic and copies ran while one was open for 11% -> 0% of each run, Pallas kernels for 0% -> 0%
where the time goes in v1:
time: 202 us; the launch traced here: 199 us
  Pallas kernels  184 us (91%)
  local copies, waits for them, and re-layouts  9.42 us (5%)
  other arithmetic  4.86 us (2%)
    pallas_call x1, Pallas kernels, expert_layer(): pl.pallas_call(kernel, out_shape=(jax.ShapeDtypeStruct((count, width), bf...  184 us
    unnamed x17, local copies, waits for them, and re-layouts  9.42 us

profile of v1, /device:TPU:32, one launch (start us, length us, event | category | flops | bytes accessed | tf_op | source)
XLA Modules:
  0.0 198.9 jit_solution(3218143129320514976)
XLA Ops:
  0.6 0.7 convert_bitcast_fusion.1
  1.4 0.8 convert_bitcast_fusion
  2.1 0.6 fusion.3.shard_ref
  2.7 0.0 copy-start
  2.7 4.7 %copy.20.gate_ref = bf16[1,2048,704]{2,1,0:T(8,128)(2,1)} copy(bf16[1,2048,704]{1,2,0:T(8,128)(2,1)} %param.17) | data formatting | bytes 5767168 | tf_op args[4]
  7.5 0.0 copy-done
  7.5 2.8 %copy.21.up_ref = bf16[1,2048,704]{2,1,0:T(8,128)(2,1)} copy(bf16[1,2048,704]{1,2,0:T(8,128)(2,1)S(1)} %copy-done) | data formatting | bytes 5767168 | tf_op args[5]
  10.2 0.0 copy-start.2
  10.3 0.0 copy-start.5
  10.3 0.0 copy-start.6
  10.3 0.0 copy-start.1
  10.3 0.0 copy-start.3
  10.3 0.0 copy-start.4
  10.3 183.9 %expert_layer.1 = (bf16[128,2048]{1,0:T(8,128)(2,1)}, f32[32,384]{1,0:T(8,128)}) custom-call(bf16[128,2048]{1,0:T(8,128)(2,1)} %tok_ref.1, bf16[128,2048]{1,0:T(8,128)(2,1)} %grad_ref.1, s32[6,128]{1,0:T(8,128)} %bitcast.65, f32[6,128]{1,0:T(8,128)} %bitcast.66, bf16[1,2048,704]{2,1,0:T(8,128)(2,1)} %copy.20.gate_ref, bf16[1,2048,704]{2,1,0:T(8,128)(2,1)} %copy.21.up_ref, ...), custom_call_target="tpu_custom_call" | custom-call | tf_op jit(solution)/shard_map/expert_layer/pallas_call | solution.py:379
  194.2 0.0 copy-done.2
  194.2 0.0 copy-done.5
  194.2 0.0 copy-done.6
  194.2 1.4 fusion.5
  195.6 0.0 copy-done.1
  195.6 0.0 copy-done.3
  195.6 0.0 copy-done.4
  195.6 1.4 fusion.2
  197.0 1.9 copy.23
Async XLA Ops:
  2.7 4.7 %copy-start = (bf16[1,2048,704]{1,2,0:T(8,128)(2,1)S(1)}, bf16[1,2048,704]{1,2,0:T(8,128)(2,1)}, u32[]{:S(2)}) copy-start(bf16[1,2048,704]{1,2,0:T(8,128)(2,1)} %param.18) | copy-start | bytes 8650756
  10.2 183.9 %copy-start.2 = (f32[1,88,32]{1,2,0:T(8,128)S(1)}, f32[1,88,32]{1,2,0:T(8,128)}, u32[]{:S(2)}) copy-start(f32[1,88,32]{1,2,0:T(8,128)} %param.20) | copy-start | bytes 33796
  10.3 183.9 %copy-start.5 = (f32[1,88,32]{1,2,0:T(8,128)S(1)}, f32[1,88,32]{1,2,0:T(8,128)}, u32[]{:S(2)}) copy-start(f32[1,88,32]{1,2,0:T(8,128)} %param.22) | copy-start | bytes 33796
  10.3 183.9 %copy-start.6 = (f32[1,88,32]{1,2,0:T(8,128)S(1)}, f32[1,88,32]{1,2,0:T(8,128)}, u32[]{:S(2)}) copy-start(f32[1,88,32]{1,2,0:T(8,128)} %param.23) | copy-start | bytes 33796
  10.3 185.3 %copy-start.1 = (f32[1,32,256]{2,1,0:T(8,128)S(1)}, f32[1,32,256]{2,1,0:T(8,128)}, u32[]{:S(2)}) copy-start(f32[1,32,256]{2,1,0:T(8,128)} %param.21) | copy-start | bytes 98308
  10.3 185.3 %copy-start.3 = (f32[1,32,256]{2,1,0:T(8,128)S(1)}, f32[1,32,256]{2,1,0:T(8,128)}, u32[]{:S(2)}) copy-start(f32[1,32,256]{2,1,0:T(8,128)} %param.24) | copy-start | bytes 98308
  10.3 185.3 %copy-start.4 = (f32[1,32,256]{2,1,0:T(8,128)S(1)}, f32[1,32,256]{2,1,0:T(8,128)}, u32[]{:S(2)}) copy-start(f32[1,32,256]{2,1,0:T(8,128)} %param.25) | copy-start | bytes 98308

commit v2 on v1

v2 whole, which is shorter than its diff:
```python
import functools
import math

import jax
import jax.numpy as jnp
from jax import lax
from jax.experimental import pallas as pl
from jax.experimental.pallas import tpu as pltpu
from jax.sharding import PartitionSpec as P

adapter_scale = 2.0
beta_one = 0.9
beta_two = 0.999
bias_one = 1.0 - math.exp(1000.0 * math.log(0.9))
bias_two = 1.0 - math.exp(1000.0 * math.log(0.999))
adam_eps = 1e-08
weight_decay = 0.1

MESH = pl.DeviceIdType.MESH
NT = (((1,), (1,)), ((), ()))
NN = (((1,), (0,)), ((), ()))
TN = (((0,), (0,)), ((), ()))
RING = 8
SLOT = 32
RANK = 32
PART = 384
f32 = jnp.float32
bf16 = jnp.bfloat16


def dot(a, b, dims=NN):
    return lax.dot_general(a, b, dims, preferred_element_type=f32)


def kernel(
    tok_ref, grad_ref, chosen_ref, weight_ref, gate_ref, up_ref, down_ref, first_ref, second_ref,
    out_ref, sum_ref,
    tg, wg, wu, wd, ab, gr, shard, ms, mr, rp, rm, factor, act, slope, hid, lg,
    ag_send, ag_recv, own_send, own_recv, w_send, w_recv, rs_send, rs_recv, ab_send, ab_recv,
    gab_send, gab_recv, m_send, m_recv, own_sem,
):
    tokens, width = tok_ref.shape
    units = gate_ref.shape[1]
    half = width // 2
    eighth = width // 8
    unit_count = units // 8
    dp = lax.axis_index("dp")
    ex = lax.axis_index("expert")
    z, xh, core = ex // 4, (ex // 2) % 2, ex % 2
    y, xl = dp // 2, dp % 2

    def at(zz, hh, cc):
        return (zz * 2 + hh) * 2 + cc

    zp = (dp, at((z + 1) % RING, xh, core))
    zm = (dp, at((z + RING - 1) % RING, xh, core))
    sib = (dp, at(z, xh, 1 - core))
    cross = (y * 2 + 1 - xl, at(z, 1 - xh, core))
    xlo = (y * 2 + 1 - xl, ex)
    yp = (((y + 1) % 4) * 2 + xl, ex)
    ym = (((y + 3) % 4) * 2 + xl, ex)

    def plane(k, j):
        hh = xh if k < 2 else 1 - xh
        cc = core if k % 2 == 0 else 1 - core
        return ((dp + j) % 8, at(z, hh, cc))

    def each_peer(f):
        for k in range(4):
            lax.fori_loop(1 if k == 0 else 0, 8, functools.partial(lambda k, j, c: (f(k, j), c)[1], k), 0)

    barrier = pltpu.get_barrier_semaphore()

    def greet(device):
        pl.semaphore_signal(barrier, inc=1, device_id=device, device_id_type=MESH)

    each_peer(lambda k, j: greet(plane(k, j)))
    lax.fori_loop(1, RING, lambda r, c: (greet((dp, at((z + r) % RING, xh, core))), c)[1], 0)
    pl.semaphore_wait(barrier, 31 + RING - 1)

    def remote(src, dst, send, recv, device):
        return pltpu.make_async_remote_copy(
            src_ref=src, dst_ref=dst, send_sem=send, recv_sem=recv, device_id=device, device_id_type=MESH
        )

    def sl(r):
        return (r + 2) % RING

    def piece(ref, h):
        return ref.at[:, pl.ds(h * half, half)]

    def ag(a, way, hop, h):
        own = tok_ref if a == 0 else grad_ref
        here = hop if way == 0 else RING - hop
        there = hop + 1 if way == 0 else RING - hop - 1
        src = own if hop == 0 else tg.at[a, sl(here)]
        return remote(
            piece(src, h), piece(tg.at[a, sl(there)], h), ag_send.at[a, way, hop, h],
            ag_recv.at[a, there, h], zp if way == 0 else zm,
        )

    def ag_has(hop, way, h):
        return hop < 3 or h == way

    def ag_own(a):
        for h in range(2):
            for way in range(2):
                ag(a, way, 0, h).start()

    def ag_arrive(a, hop, h):
        for way in range(2):
            if ag_has(hop - 1, way, h):
                ag(a, way, hop - 1, h).wait_recv()
                if hop < 4 and ag_has(hop, way, h):
                    ag(a, way, hop, h).start()

    def ag_sent(a, hops):
        for hop in hops:
            for h in range(2):
                for way in range(2):
                    if ag_has(hop, way, h):
                        ag(a, way, hop, h).wait_send()

    own_w = (gate_ref.at[0], up_ref.at[0], down_ref.at[0])
    all_w = (wg, wu, wd)
    mine = (y % 2) * 2
    other = 2 - mine

    def w_copy(i, n):
        m, j = i // 2, i % 2
        quarter = (
            mine + 1 - xl, mine + xl, mine + xl, mine + 1 - xl,
            mine + xl, mine + 1 - xl, other + xl, other + 1 - xl,
        )[n]
        cols = pl.ds(pl.multiple_of((quarter * 2 + j) * eighth, eighth), eighth)
        src = own_w[m] if n == 0 else all_w[m].at[2]
        dst = all_w[m].at[2 if n < 4 else 3]
        device = (cross, xlo, ym, yp, sib, sib, sib, sib)[n]
        return remote(src.at[:, cols], dst.at[:, cols], w_send.at[i, n], w_recv.at[i, n], device)

    def w_own(m):
        return remote(own_w[m], all_w[m].at[1], own_send.at[m], own_recv.at[m], sib)

    def w_first(i):
        w_copy(i, 0).wait_recv()
        for n in (1, 2, 4):
            w_copy(i, n).start()
        if i < 4:
            w_copy(i + 2, 0).start()

    def w_second(i):
        w_copy(i, 1).wait_recv()
        for n in (3, 5):
            w_copy(i, n).start()
        w_copy(i, 2).wait_recv()
        w_copy(i, 6).start()

    def w_third(i):
        w_copy(i, 3).wait_recv()
        w_copy(i, 7).start()

    def w_have(some):
        for i in some:
            for n in (4, 5, 6, 7):
                w_copy(i, n).wait_recv()

    ag_own(0)
    w_copy(0, 0).start()
    w_copy(1, 0).start()
    own_copies = [pltpu.make_async_copy(own_w[m], all_w[m].at[0], own_sem.at[2 + m]) for m in range(3)]
    own_tok = pltpu.make_async_copy(tok_ref, tg.at[0, sl(0)], own_sem.at[0])
    own_grad = pltpu.make_async_copy(grad_ref, tg.at[1, sl(0)], own_sem.at[1])
    own_tok.start()
    own_grad.start()
    for m in range(3):
        w_own(m).start()
        own_copies[m].start()

    shard[...] = jnp.zeros_like(shard)
    shard[:, 0:unit_count] = first_ref[0].astype(bf16)
    shard[:, 128:PART] = second_ref[0].astype(bf16)
    ab[pl.ds(dp, 1)] = shard[...][None]

    def ab_copy(k, j):
        return remote(shard, ab.at[k * 8 + dp], ab_send, ab_recv, plane(k, j))

    each_peer(lambda k, j: ab_copy(k, j).start())

    ids = lax.broadcasted_iota(jnp.int32, (4 * RING, tokens), 0)
    named = jnp.zeros((4 * RING, tokens), f32)
    weighted = jnp.zeros((4 * RING, tokens), f32)
    for k in range(chosen_ref.shape[0]):
        hit = ids == chosen_ref[k : k + 1, :]
        named = jnp.where(hit, 1.0, named)
        weighted = jnp.where(hit, weight_ref[k : k + 1, :], weighted)
    earlier = lax.broadcasted_iota(jnp.int32, (tokens, tokens), 0) < lax.broadcasted_iota(
        jnp.int32, (tokens, tokens), 1
    )
    rank = dot(named.astype(bf16), jnp.where(earlier, 1.0, 0.0).astype(bf16))
    rank = jnp.where(named > 0.5, rank, -1.0)
    for zz in range(RING):
        ms[zz, 0:4, :] = rank[zz * 4 : zz * 4 + 4]
        ms[zz, 4:8, :] = weighted[zz * 4 : zz * 4 + 4]
    mr[pl.ds(sl(0), 1)] = ms[pl.ds(z, 1)]

    def m_copy(r):
        there = (z + r) % RING
        return remote(ms.at[there], mr.at[sl(r)], m_send, m_recv, (dp, at(there, xh, core)))

    lax.fori_loop(1, RING, lambda r, c: (m_copy(r).start(), c)[1], 0)

    def spread(d):
        i = lax.broadcasted_iota(jnp.int32, (128, units), 0)
        j = lax.broadcasted_iota(jnp.int32, (128, units), 1)
        return jnp.where((j - d * unit_count == i) & (i < unit_count), 1.0, 0.0).astype(bf16)

    def assemble(d, carry):
        one = spread(d)
        for k in range(4):
            factor[k] = factor[k] + dot(ab[k * 8 + d, :, 0:128], one)
        return carry

    slots = lax.broadcasted_iota(jnp.int32, (SLOT, tokens), 0).astype(f32)

    def row_of(k):
        hh = xh if k < 2 else 1 - xh
        cc = core if k % 2 == 0 else 1 - core
        return hh * 2 + cc

    def picks(b):
        return [jnp.where(slots == mr[b, pl.ds(row_of(k), 1), :], 1.0, 0.0) for k in range(4)]

    def gather_tokens(b, carry):
        tg[0, b] = dot(jnp.concatenate(picks(b), axis=0).astype(bf16), tg[0, b]).astype(bf16)
        return carry

    def gather_grads(b, carry):
        chosen = picks(b)
        scale = jnp.concatenate(
            [
                jnp.sum(chosen[k] * mr[b, pl.ds(row_of(k) + 4, 1), :], axis=1, keepdims=True)
                for k in range(4)
            ],
            axis=0,
        )
        pick = jnp.concatenate(chosen, axis=0).astype(bf16)
        tg[1, b] = (dot(pick, tg[1, b]) * scale).astype(bf16)
        return carry

    def rows_of(k):
        return pl.ds(pl.multiple_of(k * SLOT, SLOT), SLOT)

    def forward(k, carry):
        x = tg[0, :, rows_of(k), :].reshape(RING * SLOT, width)
        gate_pre = dot(x, wg[k], NT)
        up_pre = dot(x, wu[k], NT)
        s = jax.nn.sigmoid(gate_pre)
        activated = gate_pre * s
        act[k] = activated
        hid[k] = (activated * up_pre).astype(bf16)
        slope[k] = up_pre * s * (1.0 + gate_pre * (1.0 - s))
        return carry

    def second_factor(k):
        return jnp.concatenate([ab[k * 8 + d, :, 128:PART] for d in range(8)], axis=1)

    def backward(first, blocks):
        rows = slice(first * SLOT, (first + blocks) * SLOT)
        near = slice(first, first + blocks)

        def one(k, carry):
            g = tg[1, near, rows_of(k), :].reshape(blocks * SLOT, width)
            low_grad = dot(g, second_factor(k), NT).astype(bf16)
            lg[k, rows, :] = low_grad
            hidden_grad = dot(g, wd[k], NT) + adapter_scale * dot(low_grad, factor[k].astype(bf16))
            gate_grad = (hidden_grad * slope[k, rows, :]).astype(bf16)
            up_grad = (hidden_grad * act[k, rows, :]).astype(bf16)
            pair = dot(gate_grad, wg[k]) + dot(up_grad, wu[k])
            tg[0, near, rows_of(k), :] = pair.astype(bf16).reshape(blocks, SLOT, width)
            return carry

        return one

    def combine(b, carry):
        pick = jnp.concatenate(picks(b), axis=0).astype(bf16)
        tg[0, b] = dot(pick, tg[0, b], TN).astype(bf16)
        return carry

    def adapter_grads(k, carry):
        g = tg[1, :, rows_of(k), :].reshape(RING * SLOT, width)
        low_rank = dot(hid[k], factor[k].astype(bf16), NT).astype(bf16)
        grad_a = (adapter_scale * dot(lg[k], hid[k], TN)).astype(bf16)
        grad_b = (adapter_scale * dot(low_rank, g, TN)).astype(bf16)
        for d in range(8):
            ab[k * 8 + d, :, 0:128] = dot(grad_a, spread(d), NT).astype(bf16)
            ab[k * 8 + d, :, 128:PART] = grad_b[:, d * 256 : d * 256 + 256]
        return carry

    ag_arrive(0, 1, 0)
    w_first(0)
    ag_arrive(0, 1, 1)
    w_first(1)
    ag_arrive(0, 2, 0)
    w_second(0)
    w_first(2)
    ag_arrive(0, 2, 1)
    many = ab.at[pl.ds(0, 31)]
    pltpu.make_async_copy(many, many, ab_recv).wait()
    pltpu.make_async_copy(many, many, ab_send).wait()
    factor[...] = jnp.zeros_like(factor)
    lax.fori_loop(0, 4, assemble, 0)
    w_second(1)
    ag_arrive(0, 3, 0)
    ag_own(1)
    w_third(0)
    w_first(3)
    lax.fori_loop(4, 8, assemble, 0)
    ag_arrive(0, 3, 1)
    w_second(2)
    w_third(1)
    seven = mr.at[pl.ds(0, RING - 1)]
    pltpu.make_async_copy(seven, seven, m_recv).wait()
    pltpu.make_async_copy(seven, seven, m_send).wait()
    own_tok.wait()
    own_grad.wait()
    ag_arrive(0, 4, 0)
    ag_arrive(0, 4, 1)

    w_first(4)
    w_second(3)
    w_third(2)
    ag_sent(0, range(4))
    ag_arrive(1, 1, 0)
    lax.fori_loop(0, RING, gather_tokens, 0)
    for m in range(3):
        own_copies[m].wait()
        w_own(m).wait_recv()
    w_first(5)
    w_second(4)
    w_third(3)
    ag_arrive(1, 1, 1)
    lax.fori_loop(0, 2, forward, 0)
    ag_arrive(1, 2, 0)
    w_have((0, 1, 2, 3))
    w_second(5)
    w_third(4)
    lax.fori_loop(2, 4, forward, 0)
    ag_arrive(1, 2, 1)
    w_third(5)
    ag_sent(1, (1, 2))
    lax.fori_loop(0, 5, gather_grads, 0)
    ag_arrive(1, 3, 0)
    lax.fori_loop(0, 2, backward(0, 5), 0)
    ag_arrive(1, 3, 1)
    w_have((4, 5))
    lax.fori_loop(2, 4, backward(0, 5), 0)
    ag_arrive(1, 4, 0)
    ag_arrive(1, 4, 1)
    ag_sent(1, (0, 3))
    lax.fori_loop(5, RING, gather_grads, 0)
    lax.fori_loop(0, 4, backward(5, 3), 0)
    lax.fori_loop(5, RING, combine, 0)

    def landing(way, step, h):
        return (rp if way == 0 else rm).at[0 if step == 0 else 2 * step - 1 + h]

    def rs(way, step, h):
        here = 4 + step if way == 0 else 4 - step
        return remote(
            piece(tg.at[0, sl(here)], h), landing(way, step, h), rs_send.at[way, step, h],
            rs_recv.at[way, step, h], zp if way == 0 else zm,
        )

    def rs_add(way, step, h):
        rs(way, step, h).wait_recv()
        here = sl(5 + step if way == 0 else 3 - step)
        cols = slice(h * half, h * half + half)
        tg[0, here, :, cols] = (
            tg[0, here, :, cols].astype(f32) + landing(way, step, h)[...].astype(f32)
        ).astype(bf16)
        rs(way, step + 1, h).start()

    for way in range(2):
        rs(way, 0, way).start()
        rs(way, 1, 1 - way).start()
    lax.fori_loop(0, 5, combine, 0)
    for way in range(2):
        rs_add(way, 0, way)
    lax.fori_loop(0, 2, adapter_grads, 0)
    for way in range(2):
        rs_add(way, 1, 1 - way)
    lax.fori_loop(2, 4, adapter_grads, 0)

    def gab_copy(k, j):
        return remote(ab.at[k * 8 + (dp + j) % 8], gr.at[k * 8 + dp], gab_send, gab_recv, plane(k, j))

    each_peer(lambda k, j: gab_copy(k, j).start())
    for way in range(2):
        rs_add(way, 1, way)
    for way in range(2):
        rs_add(way, 2, 1 - way)
    for way in range(2):
        rs_add(way, 2, way)

    many_g = gr.at[pl.ds(0, 31)]
    pltpu.make_async_copy(many_g, many_g, gab_recv).wait()
    pltpu.make_async_copy(many_g, many_g, gab_send).wait()
    gr[pl.ds(dp, 1)] = ab[pl.ds(dp, 1)]
    sum_ref[...] = lax.fori_loop(
        0, 32, lambda i, total: total + gr[i].astype(f32), jnp.zeros((RANK, PART), f32)
    )
    for i in range(6):
        for n in range(8):
            w_copy(i, n).wait_send()
    for m in range(3):
        w_own(m).wait_send()
    for h in (1, 0):
        rs(0, 3, h).wait_recv()
        rs(1, 3, h).wait_recv()
        cols = slice(h * half, h * half + half)
        out_ref[:, cols] = (
            tg[0, sl(0), :, cols].astype(f32)
            + landing(0, 3, h)[...].astype(f32)
            + landing(1, 3, h)[...].astype(f32)
        ).astype(bf16)
    for way in range(2):
        for step in range(4):
            for h in range(2):
                if step > 0 or h == way:
                    rs(way, step, h).wait_send()


def expert_layer(tokens, grads, chosen, weights, gate, up, down, first, second):
    count, width = tokens.shape
    units = gate.shape[1]
    rows = RING * SLOT
    vmem = pl.BlockSpec(memory_space=pltpu.VMEM)
    hbm = pl.BlockSpec(memory_space=pl.ANY)
    dma = pltpu.SemaphoreType.DMA
    return pl.pallas_call(
        kernel,
        out_shape=(
            jax.ShapeDtypeStruct((count, width), bf16),
            jax.ShapeDtypeStruct((RANK, PART), f32),
        ),
        in_specs=[hbm, hbm, vmem, vmem, hbm, hbm, hbm, vmem, vmem],
        out_specs=(vmem, vmem),
        scratch_shapes=[
            pltpu.VMEM((2, RING, count, width), bf16),
            pltpu.VMEM((4, units, width), bf16),
            pltpu.VMEM((4, units, width), bf16),
            pltpu.VMEM((4, units, width), bf16),
            pltpu.VMEM((32, RANK, PART), bf16),
            pltpu.VMEM((32, RANK, PART), bf16),
            pltpu.VMEM((RANK, PART), bf16),
            pltpu.VMEM((RING, 8, count), f32),
            pltpu.VMEM((RING, 8, count), f32),
            pltpu.VMEM((7, count, width // 2), bf16),
            pltpu.VMEM((7, count, width // 2), bf16),
            pltpu.VMEM((4, RANK, units), f32),
            pltpu.VMEM((4, rows, units), f32),
            pltpu.VMEM((4, rows, units), f32),
            pltpu.VMEM((4, rows, units), bf16),
            pltpu.VMEM((4, rows, RANK), bf16),
            dma((2, 2, 4, 2)),
            dma((2, 8, 2)),
            dma((3,)),
            dma((3,)),
            dma((6, 8)),
            dma((6, 8)),
            dma((2, 4, 2)),
            dma((2, 4, 2)),
            dma,
            dma,
            dma,
            dma,
            dma,
            dma,
            dma((5,)),
        ],
        compiler_params=pltpu.CompilerParams(
            collective_id=0, has_side_effects=True, vmem_limit_bytes=60 * 1024 * 1024
        ),
        name="expert_layer",
    )(tokens, grads, chosen, weights, gate, up, down, first, second)


def decoupled_adam_update(param, grad, moment, second):
    moment_new = beta_one * moment + (1.0 - beta_one) * grad
    second_new = beta_two * second + (1.0 - beta_two) * grad * grad
    update = (
        moment_new / bias_one / (jnp.sqrt(second_new / bias_two) + adam_eps) + weight_decay * param
    )
    return (moment_new, second_new, update)


def shards(
    tokens,
    output_gradient,
    chosen_expert_index,
    router_weight,
    gate_weight,
    up_weight,
    down_weight,
    adapter_down_first,
    adapter_down_second,
    first_mean_a,
    squared_mean_a,
    first_mean_b,
    squared_mean_b,
):
    unit_count = adapter_down_first.shape[1]
    token_grad, sums = expert_layer(
        tokens,
        output_gradient,
        chosen_expert_index.T,
        router_weight.T,
        jnp.swapaxes(gate_weight, 1, 2),
        jnp.swapaxes(up_weight, 1, 2),
        down_weight,
        jnp.swapaxes(adapter_down_first, 1, 2),
        adapter_down_second,
    )
    updated_a = decoupled_adam_update(
        adapter_down_first[0], sums[:, :unit_count].T, first_mean_a[0], squared_mean_a[0]
    )
    updated_b = decoupled_adam_update(
        adapter_down_second[0], sums[:, 128:], first_mean_b[0], squared_mean_b[0]
    )
    return (token_grad, *(v[None] for v in updated_a), *(v[None] for v in updated_b))


def solution(mesh):
    rows = P(("dp", "expert"), None)
    frozen = P("expert", None, None)
    first = P("expert", "dp", None)
    second = P("expert", None, "dp")
    return jax.shard_map(
        shards,
        mesh=mesh,
        in_specs=(rows,) * 4 + (frozen,) * 3 + (first, second, first, first, second, second),
        out_specs=(rows, first, first, first, second, second, second),
        check_vma=False,
    )
```

time: 202 us -> 168 us (0.83)
  Pallas kernels: 184 us -> 161 us
  local copies, waits for them, and re-layouts: 9.42 us -> 1.91 us
  other arithmetic: 4.86 us -> 2.76 us
    pallas_call x1, Pallas kernels: 184 us -> 161 us  [expert_layer(): pl.pallas_call(kernel, out_shape=(jax.ShapeDtypeStruct((count, width), bf...]
    unnamed x17 -> x13, local copies, waits for them, and re-layouts: 9.42 us -> 1.91 us
where the time goes in v2:
time: 168 us; the launch traced here: 167 us
  Pallas kernels  161 us (96%)
  other arithmetic  2.76 us (2%)
  local copies, waits for them, and re-layouts  1.91 us (1%)
    pallas_call x1, Pallas kernels, expert_layer(): pl.pallas_call(kernel, out_shape=(jax.ShapeDtypeStruct((count, width), bf...  161 us

profile of v2, /device:TPU:32, one launch (start us, length us, event | category | flops | bytes accessed | tf_op | source)
XLA Modules:
  0.0 166.5 jit_solution(11196232176361216152)
XLA Ops:
  0.6 0.0 copy-start.1
  0.6 0.0 copy-start.4
  0.7 0.0 copy-start.5
  0.7 0.0 copy-start
  0.7 0.0 copy-start.2
  0.7 0.0 copy-start.3
  0.7 161.1 %expert_layer.1 = (bf16[128,2048]{1,0:T(8,128)(2,1)}, f32[32,384]{1,0:T(8,128)}) custom-call(bf16[128,2048]{1,0:T(8,128)(2,1)} %tok_ref.1, bf16[128,2048]{1,0:T(8,128)(2,1)} %grad_ref.1, s32[6,128]{1,0:T(8,128)} %bitcast.65, f32[6,128]{1,0:T(8,128)} %bitcast.66, bf16[1,704,2048]{2,1,0:T(8,128)(2,1)} %bitcast.62, bf16[1,704,2048]{2,1,0:T(8,128)(2,1)} %bitcast.63, ...), custom_call_target="tpu_custom_call" | custom-call | tf_op jit(solution)/shard_map/expert_layer/pallas_call | solution.py:440
  161.8 0.0 copy-done.1
  161.8 0.0 copy-done.4
  161.9 0.0 copy-done.5
  161.9 1.4 fusion.3
  163.2 0.0 copy-done
  163.2 0.0 copy-done.2
  163.2 0.0 copy-done.3
  163.2 1.4 fusion.1
  164.6 1.9 %copy.21 = bf16[128,2048]{1,0:T(8,128)(2,1)} copy(bf16[128,2048]{1,0:T(8,128)(2,1)} %get-tuple-element.24) | data formatting | bytes 1048576
Async XLA Ops:
  0.6 161.2 %copy-start.1 = (f32[1,88,32]{1,2,0:T(8,128)S(1)}, f32[1,88,32]{1,2,0:T(8,128)}, u32[]{:S(2)}) copy-start(f32[1,88,32]{1,2,0:T(8,128)} %param.20) | copy-start | bytes 33796
  0.6 161.2 %copy-start.4 = (f32[1,88,32]{1,2,0:T(8,128)S(1)}, f32[1,88,32]{1,2,0:T(8,128)}, u32[]{:S(2)}) copy-start(f32[1,88,32]{1,2,0:T(8,128)} %param.22) | copy-start | bytes 33796
  0.7 161.2 %copy-start.5 = (f32[1,88,32]{1,2,0:T(8,128)S(1)}, f32[1,88,32]{1,2,0:T(8,128)}, u32[]{:S(2)}) copy-start(f32[1,88,32]{1,2,0:T(8,128)} %param.23) | copy-start | bytes 33796
  0.7 162.6 %copy-start = (f32[1,32,256]{2,1,0:T(8,128)S(1)}, f32[1,32,256]{2,1,0:T(8,128)}, u32[]{:S(2)}) copy-start(f32[1,32,256]{2,1,0:T(8,128)} %second_ref.1) | copy-start | bytes 98308
  0.7 162.5 %copy-start.2 = (f32[1,32,256]{2,1,0:T(8,128)S(1)}, f32[1,32,256]{2,1,0:T(8,128)}, u32[]{:S(2)}) copy-start(f32[1,32,256]{2,1,0:T(8,128)} %param.24) | copy-start | bytes 98308
  0.7 162.5 %copy-start.3 = (f32[1,32,256]{2,1,0:T(8,128)S(1)}, f32[1,32,256]{2,1,0:T(8,128)}, u32[]{:S(2)}) copy-start(f32[1,32,256]{2,1,0:T(8,128)} %param.25) | copy-start | bytes 98308

commit v3 on v2

--- a/solution.py
+++ b/solution.py
@@ -184,7 +184,6 @@
     def ab_copy(k, j):
         return remote(shard, ab.at[k * 8 + dp], ab_send, ab_recv, plane(k, j))
 
-    each_peer(lambda k, j: ab_copy(k, j).start())
 
     ids = lax.broadcasted_iota(jnp.int32, (4 * RING, tokens), 0)
     named = jnp.zeros((4 * RING, tokens), f32)
@@ -281,6 +280,35 @@
 
         return one
 
+    far = slice(5 * SLOT, RING * SLOT)
+
+    def far_slopes(k, carry):
+        g = tg[1, 5:RING, rows_of(k), :].reshape(3 * SLOT, width)
+        low_grad = dot(g, second_factor(k), NT).astype(bf16)
+        lg[k, far, :] = low_grad
+        hidden_grad = dot(g, wd[k], NT) + adapter_scale * dot(low_grad, factor[k].astype(bf16))
+        slope[k, far, :] = (hidden_grad * slope[k, far, :]).astype(bf16).astype(f32)
+        act[k, far, :] = (hidden_grad * act[k, far, :]).astype(bf16).astype(f32)
+        return carry
+
+    def far_pairs(h):
+        cols = slice(h * half, h * half + half)
+
+        def one(k, carry):
+            pair = dot(slope[k, far, :].astype(bf16), wg[k, :, cols]) + dot(
+                act[k, far, :].astype(bf16), wu[k, :, cols]
+            )
+            tg[0, 5:RING, rows_of(k), cols] = pair.astype(bf16).reshape(3, SLOT, half)
+            return carry
+
+        def sums(b, carry):
+            pick = jnp.concatenate(picks(b), axis=0).astype(bf16)
+            tg[0, b, :, cols] = dot(pick, tg[0, b, :, cols], TN).astype(bf16)
+            return carry
+
+        lax.fori_loop(0, 4, one, 0)
+        lax.fori_loop(5, RING, sums, 0)
+
     def combine(b, carry):
         pick = jnp.concatenate(picks(b), axis=0).astype(bf16)
         tg[0, b] = dot(pick, tg[0, b], TN).astype(bf16)
@@ -302,53 +330,53 @@
     w_first(1)
     ag_arrive(0, 2, 0)
     w_second(0)
+    ag_arrive(0, 2, 1)
     w_first(2)
-    ag_arrive(0, 2, 1)
+    each_peer(lambda k, j: ab_copy(k, j).start())
+    w_second(1)
+    ag_arrive(0, 3, 0)
+    w_third(0)
+    ag_arrive(0, 3, 1)
+    ag_own(1)
+    w_first(3)
+    w_second(2)
+    own_tok.wait()
+    own_grad.wait()
+    seven = mr.at[pl.ds(0, RING - 1)]
+    pltpu.make_async_copy(seven, seven, m_recv).wait()
+    pltpu.make_async_copy(seven, seven, m_send).wait()
+    ag_arrive(0, 4, 0)
+    ag_arrive(0, 4, 1)
+
+    w_third(1)
+    w_first(4)
+    w_second(3)
+    ag_sent(0, range(4))
+    ag_arrive(1, 1, 0)
+    w_third(2)
+    lax.fori_loop(0, RING, gather_tokens, 0)
+    w_first(5)
+    ag_arrive(1, 1, 1)
+    for m in range(3):
+        own_copies[m].wait()
+        w_own(m).wait_recv()
+    lax.fori_loop(0, 2, forward, 0)
+    w_second(4)
+    w_third(3)
+    ag_arrive(1, 2, 0)
+    w_have((0, 1, 2, 3))
+    lax.fori_loop(2, 4, forward, 0)
+    w_second(5)
+    w_third(4)
+    ag_arrive(1, 2, 1)
     many = ab.at[pl.ds(0, 31)]
     pltpu.make_async_copy(many, many, ab_recv).wait()
     pltpu.make_async_copy(many, many, ab_send).wait()
     factor[...] = jnp.zeros_like(factor)
-    lax.fori_loop(0, 4, assemble, 0)
-    w_second(1)
-    ag_arrive(0, 3, 0)
-    ag_own(1)
-    w_third(0)
-    w_first(3)
-    lax.fori_loop(4, 8, assemble, 0)
-    ag_arrive(0, 3, 1)
-    w_second(2)
-    w_third(1)
-    seven = mr.at[pl.ds(0, RING - 1)]
-    pltpu.make_async_copy(seven, seven, m_recv).wait()
-    pltpu.make_async_copy(seven, seven, m_send).wait()
-    own_tok.wait()
-    own_grad.wait()
-    ag_arrive(0, 4, 0)
-    ag_arrive(0, 4, 1)
-
-    w_first(4)
-    w_second(3)
-    w_third(2)
-    ag_sent(0, range(4))
-    ag_arrive(1, 1, 0)
-    lax.fori_loop(0, RING, gather_tokens, 0)
-    for m in range(3):
-        own_copies[m].wait()
-        w_own(m).wait_recv()
-    w_first(5)
-    w_second(4)
-    w_third(3)
-    ag_arrive(1, 1, 1)
-    lax.fori_loop(0, 2, forward, 0)
-    ag_arrive(1, 2, 0)
-    w_have((0, 1, 2, 3))
-    w_second(5)
-    w_third(4)
-    lax.fori_loop(2, 4, forward, 0)
-    ag_arrive(1, 2, 1)
-    w_third(5)
+    lax.fori_loop(0, 8, assemble, 0)
     ag_sent(1, (1, 2))
     lax.fori_loop(0, 5, gather_grads, 0)
+    w_third(5)
     ag_arrive(1, 3, 0)
     lax.fori_loop(0, 2, backward(0, 5), 0)
     ag_arrive(1, 3, 1)
@@ -358,8 +386,7 @@
     ag_arrive(1, 4, 1)
     ag_sent(1, (0, 3))
     lax.fori_loop(5, RING, gather_grads, 0)
-    lax.fori_loop(0, 4, backward(5, 3), 0)
-    lax.fori_loop(5, RING, combine, 0)
+    lax.fori_loop(0, 4, far_slopes, 0)
 
     def landing(way, step, h):
         return (rp if way == 0 else rm).at[0 if step == 0 else 2 * step - 1 + h]
@@ -380,9 +407,10 @@
         ).astype(bf16)
         rs(way, step + 1, h).start()
 
-    for way in range(2):
-        rs(way, 0, way).start()
-        rs(way, 1, 1 - way).start()
+    for h in range(2):
+        far_pairs(h)
+        rs(h, 0, h).start()
+        rs(1 - h, 1, h).start()
     lax.fori_loop(0, 5, combine, 0)
     for way in range(2):
         rs_add(way, 0, way)

time: 168 us -> 161 us (0.958)
  Pallas kernels: 161 us -> 155 us
    pallas_call x1, Pallas kernels: 161 us -> 155 us  [expert_layer(): pl.pallas_call(kernel, out_shape=(jax.ShapeDtypeStruct((count, width), bf...]
where the time goes in v3:
time: 161 us; the launch traced here: 160 us
  Pallas kernels  155 us (96%)
  other arithmetic  2.76 us (2%)
  local copies, waits for them, and re-layouts  1.91 us (1%)
    pallas_call x1, Pallas kernels, expert_layer(): pl.pallas_call(kernel, out_shape=(jax.ShapeDtypeStruct((count, width), bf...  155 us

profile of v3, /device:TPU:32, one launch (start us, length us, event | category | flops | bytes accessed | tf_op | source)
XLA Modules:
  0.0 160.2 jit_solution(13822750039203031332)
XLA Ops:
  0.6 0.0 copy-start.1
  0.6 0.0 copy-start.4
  0.7 0.0 copy-start.5
  0.7 0.0 copy-start
  0.7 0.0 copy-start.2
  0.7 0.0 copy-start.3
  0.7 154.9 %expert_layer.1 = (bf16[128,2048]{1,0:T(8,128)(2,1)}, f32[32,384]{1,0:T(8,128)}) custom-call(bf16[128,2048]{1,0:T(8,128)(2,1)} %tok_ref.1, bf16[128,2048]{1,0:T(8,128)(2,1)} %grad_ref.1, s32[6,128]{1,0:T(8,128)} %bitcast.65, f32[6,128]{1,0:T(8,128)} %bitcast.66, bf16[1,704,2048]{2,1,0:T(8,128)(2,1)} %bitcast.62, bf16[1,704,2048]{2,1,0:T(8,128)(2,1)} %bitcast.63, ...), custom_call_target="tpu_custom_call" | custom-call | tf_op jit(solution)/shard_map/expert_layer/pallas_call | solution.py:468
  155.6 0.0 copy-done.1
  155.6 0.0 copy-done.4
  155.6 0.0 copy-done.5
  155.6 1.4 fusion.3
  156.9 0.0 copy-done
  156.9 0.0 copy-done.2
  156.9 0.0 copy-done.3
  156.9 1.4 fusion.1
  158.4 1.9 %copy.21 = bf16[128,2048]{1,0:T(8,128)(2,1)} copy(bf16[128,2048]{1,0:T(8,128)(2,1)} %get-tuple-element.24) | data formatting | bytes 1048576
Async XLA Ops:
  0.6 154.9 %copy-start.1 = (f32[1,88,32]{1,2,0:T(8,128)S(1)}, f32[1,88,32]{1,2,0:T(8,128)}, u32[]{:S(2)}) copy-start(f32[1,88,32]{1,2,0:T(8,128)} %param.20) | copy-start | bytes 33796
  0.6 154.9 %copy-start.4 = (f32[1,88,32]{1,2,0:T(8,128)S(1)}, f32[1,88,32]{1,2,0:T(8,128)}, u32[]{:S(2)}) copy-start(f32[1,88,32]{1,2,0:T(8,128)} %param.22) | copy-start | bytes 33796
  0.7 154.9 %copy-start.5 = (f32[1,88,32]{1,2,0:T(8,128)S(1)}, f32[1,88,32]{1,2,0:T(8,128)}, u32[]{:S(2)}) copy-start(f32[1,88,32]{1,2,0:T(8,128)} %param.23) | copy-start | bytes 33796
  0.7 156.3 %copy-start = (f32[1,32,256]{2,1,0:T(8,128)S(1)}, f32[1,32,256]{2,1,0:T(8,128)}, u32[]{:S(2)}) copy-start(f32[1,32,256]{2,1,0:T(8,128)} %second_ref.1) | copy-start | bytes 98308
  0.7 156.3 %copy-start.2 = (f32[1,32,256]{2,1,0:T(8,128)S(1)}, f32[1,32,256]{2,1,0:T(8,128)}, u32[]{:S(2)}) copy-start(f32[1,32,256]{2,1,0:T(8,128)} %param.24) | copy-start | bytes 98308
  0.7 156.3 %copy-start.3 = (f32[1,32,256]{2,1,0:T(8,128)S(1)}, f32[1,32,256]{2,1,0:T(8,128)}, u32[]{:S(2)}) copy-start(f32[1,32,256]{2,1,0:T(8,128)} %param.25) | copy-start | bytes 98308

commit v4 on v3

--- a/solution.py
+++ b/solution.py
@@ -246,7 +246,13 @@
         tg[1, b] = (dot(pick, tg[1, b]) * scale).astype(bf16)
         return carry
 
+    def over(begin, end, f):
+        for k in range(begin, end):
+            f(k, 0)
+
     def rows_of(k):
+        if isinstance(k, int):
+            return slice(k * SLOT, (k + 1) * SLOT)
         return pl.ds(pl.multiple_of(k * SLOT, SLOT), SLOT)
 
     def forward(k, carry):
@@ -306,8 +312,8 @@
             tg[0, b, :, cols] = dot(pick, tg[0, b, :, cols], TN).astype(bf16)
             return carry
 
-        lax.fori_loop(0, 4, one, 0)
-        lax.fori_loop(5, RING, sums, 0)
+        over(0, 4, one)
+        over(5, RING, sums)
 
     def combine(b, carry):
         pick = jnp.concatenate(picks(b), axis=0).astype(bf16)
@@ -360,12 +366,12 @@
     for m in range(3):
         own_copies[m].wait()
         w_own(m).wait_recv()
-    lax.fori_loop(0, 2, forward, 0)
+    over(0, 2, forward)
     w_second(4)
     w_third(3)
     ag_arrive(1, 2, 0)
     w_have((0, 1, 2, 3))
-    lax.fori_loop(2, 4, forward, 0)
+    over(2, 4, forward)
     w_second(5)
     w_third(4)
     ag_arrive(1, 2, 1)
@@ -378,15 +384,15 @@
     lax.fori_loop(0, 5, gather_grads, 0)
     w_third(5)
     ag_arrive(1, 3, 0)
-    lax.fori_loop(0, 2, backward(0, 5), 0)
+    over(0, 2, backward(0, 5))
     ag_arrive(1, 3, 1)
     w_have((4, 5))
-    lax.fori_loop(2, 4, backward(0, 5), 0)
+    over(2, 4, backward(0, 5))
     ag_arrive(1, 4, 0)
     ag_arrive(1, 4, 1)
     ag_sent(1, (0, 3))
-    lax.fori_loop(5, RING, gather_grads, 0)
-    lax.fori_loop(0, 4, far_slopes, 0)
+    over(5, RING, gather_grads)
+    over(0, 4, far_slopes)
 
     def landing(way, step, h):
         return (rp if way == 0 else rm).at[0 if step == 0 else 2 * step - 1 + h]

time: 161 us -> 157 us (0.975)
  Pallas kernels: 155 us -> 151 us
    pallas_call x1, Pallas kernels: 155 us -> 151 us  [expert_layer(): pl.pallas_call(kernel, out_shape=(jax.ShapeDtypeStruct((count, width), bf...]
where the time goes in v4:
time: 157 us; the launch traced here: 156 us
  Pallas kernels  151 us (96%)
  other arithmetic  2.76 us (2%)
  local copies, waits for them, and re-layouts  1.91 us (1%)
    pallas_call x1, Pallas kernels, expert_layer(): pl.pallas_call(kernel, out_shape=(jax.ShapeDtypeStruct((count, width), bf...  151 us

profile of v4, /device:TPU:32, one launch (start us, length us, event | category | flops | bytes accessed | tf_op | source)
XLA Modules:
  0.0 156.2 jit_solution(5856945829472812877)
XLA Ops:
  0.6 0.0 copy-start.1
  0.6 0.0 copy-start.4
  0.7 0.0 copy-start.5
  0.7 0.0 copy-start
  0.7 0.0 copy-start.2
  0.7 0.0 copy-start.3
  0.7 150.8 %expert_layer.1 = (bf16[128,2048]{1,0:T(8,128)(2,1)}, f32[32,384]{1,0:T(8,128)}) custom-call(bf16[128,2048]{1,0:T(8,128)(2,1)} %tok_ref.1, bf16[128,2048]{1,0:T(8,128)(2,1)} %grad_ref.1, s32[6,128]{1,0:T(8,128)} %bitcast.65, f32[6,128]{1,0:T(8,128)} %bitcast.66, bf16[1,704,2048]{2,1,0:T(8,128)(2,1)} %bitcast.62, bf16[1,704,2048]{2,1,0:T(8,128)(2,1)} %bitcast.63, ...), custom_call_target="tpu_custom_call" | custom-call | tf_op jit(solution)/shard_map/expert_layer/pallas_call | solution.py:474
  151.5 0.0 copy-done.1
  151.5 0.0 copy-done.4
  151.6 0.0 copy-done.5
  151.6 1.4 fusion.3
  152.9 0.0 copy-done
  152.9 0.0 copy-done.2
  152.9 0.0 copy-done.3
  152.9 1.4 fusion.1
  154.3 1.9 %copy.21 = bf16[128,2048]{1,0:T(8,128)(2,1)} copy(bf16[128,2048]{1,0:T(8,128)(2,1)} %get-tuple-element.24) | data formatting | bytes 1048576
Async XLA Ops:
  0.6 150.9 %copy-start.1 = (f32[1,88,32]{1,2,0:T(8,128)S(1)}, f32[1,88,32]{1,2,0:T(8,128)}, u32[]{:S(2)}) copy-start(f32[1,88,32]{1,2,0:T(8,128)} %param.20) | copy-start | bytes 33796
  0.6 150.9 %copy-start.4 = (f32[1,88,32]{1,2,0:T(8,128)S(1)}, f32[1,88,32]{1,2,0:T(8,128)}, u32[]{:S(2)}) copy-start(f32[1,88,32]{1,2,0:T(8,128)} %param.22) | copy-start | bytes 33796
  0.7 150.9 %copy-start.5 = (f32[1,88,32]{1,2,0:T(8,128)S(1)}, f32[1,88,32]{1,2,0:T(8,128)}, u32[]{:S(2)}) copy-start(f32[1,88,32]{1,2,0:T(8,128)} %param.23) | copy-start | bytes 33796
  0.7 152.3 %copy-start = (f32[1,32,256]{2,1,0:T(8,128)S(1)}, f32[1,32,256]{2,1,0:T(8,128)}, u32[]{:S(2)}) copy-start(f32[1,32,256]{2,1,0:T(8,128)} %second_ref.1) | copy-start | bytes 98308
  0.7 152.2 %copy-start.2 = (f32[1,32,256]{2,1,0:T(8,128)S(1)}, f32[1,32,256]{2,1,0:T(8,128)}, u32[]{:S(2)}) copy-start(f32[1,32,256]{2,1,0:T(8,128)} %param.24) | copy-start | bytes 98308
  0.7 152.2 %copy-start.3 = (f32[1,32,256]{2,1,0:T(8,128)S(1)}, f32[1,32,256]{2,1,0:T(8,128)}, u32[]{:S(2)}) copy-start(f32[1,32,256]{2,1,0:T(8,128)} %param.25) | copy-start | bytes 98308

commit v5 on v4

--- a/solution.py
+++ b/solution.py
@@ -249,6 +249,13 @@
     def over(begin, end, f):
         for k in range(begin, end):
             f(k, 0)
+
+    def pairwise(f):
+        def two(i, carry):
+            f(2 * i, 0)
+            return f(2 * i + 1, carry)
+
+        return two
 
     def rows_of(k):
         if isinstance(k, int):
@@ -360,7 +367,7 @@
     ag_sent(0, range(4))
     ag_arrive(1, 1, 0)
     w_third(2)
-    lax.fori_loop(0, RING, gather_tokens, 0)
+    lax.fori_loop(0, RING // 2, pairwise(gather_tokens), 0)
     w_first(5)
     ag_arrive(1, 1, 1)
     for m in range(3):
@@ -381,7 +388,8 @@
     factor[...] = jnp.zeros_like(factor)
     lax.fori_loop(0, 8, assemble, 0)
     ag_sent(1, (1, 2))
-    lax.fori_loop(0, 5, gather_grads, 0)
+    lax.fori_loop(0, 2, pairwise(gather_grads), 0)
+    gather_grads(4, 0)
     w_third(5)
     ag_arrive(1, 3, 0)
     over(0, 2, backward(0, 5))
@@ -417,7 +425,8 @@
         far_pairs(h)
         rs(h, 0, h).start()
         rs(1 - h, 1, h).start()
-    lax.fori_loop(0, 5, combine, 0)
+    lax.fori_loop(0, 2, pairwise(combine), 0)
+    combine(4, 0)
     for way in range(2):
         rs_add(way, 0, way)
     lax.fori_loop(0, 2, adapter_grads, 0)

time: 157 us -> 157 us (level)
  no operation moved by 1% of the time
where the time goes in v5:
time: 157 us; the launch traced here: 156 us
  Pallas kernels  151 us (96%)
  other arithmetic  2.76 us (2%)
  local copies, waits for them, and re-layouts  1.91 us (1%)
    pallas_call x1, Pallas kernels, expert_layer(): pl.pallas_call(kernel, out_shape=(jax.ShapeDtypeStruct((count, width), bf...  151 us

profile of v5, /device:TPU:32, one launch (start us, length us, event | category | flops | bytes accessed | tf_op | source)
XLA Modules:
  0.0 156.3 jit_solution(8893217497336094005)
XLA Ops:
  0.6 0.0 copy-start.1
  0.6 0.0 copy-start.4
  0.7 0.0 copy-start.5
  0.7 0.0 copy-start
  0.7 0.0 copy-start.2
  0.7 0.0 copy-start.3
  0.7 150.9 %expert_layer.1 = (bf16[128,2048]{1,0:T(8,128)(2,1)}, f32[32,384]{1,0:T(8,128)}) custom-call(bf16[128,2048]{1,0:T(8,128)(2,1)} %tok_ref.1, bf16[128,2048]{1,0:T(8,128)(2,1)} %grad_ref.1, s32[6,128]{1,0:T(8,128)} %bitcast.65, f32[6,128]{1,0:T(8,128)} %bitcast.66, bf16[1,704,2048]{2,1,0:T(8,128)(2,1)} %bitcast.62, bf16[1,704,2048]{2,1,0:T(8,128)(2,1)} %bitcast.63, ...), custom_call_target="tpu_custom_call" | custom-call | tf_op jit(solution)/shard_map/expert_layer/pallas_call | solution.py:483
  151.6 0.0 copy-done.1
  151.6 0.0 copy-done.4
  151.6 0.0 copy-done.5
  151.6 1.4 fusion.3
  153.0 0.0 copy-done
  153.0 0.0 copy-done.2
  153.0 0.0 copy-done.3
  153.0 1.4 fusion.1
  154.4 1.9 %copy.21 = bf16[128,2048]{1,0:T(8,128)(2,1)} copy(bf16[128,2048]{1,0:T(8,128)(2,1)} %get-tuple-element.24) | data formatting | bytes 1048576
Async XLA Ops:
  0.6 151.0 %copy-start.1 = (f32[1,88,32]{1,2,0:T(8,128)S(1)}, f32[1,88,32]{1,2,0:T(8,128)}, u32[]{:S(2)}) copy-start(f32[1,88,32]{1,2,0:T(8,128)} %param.20) | copy-start | bytes 33796
  0.6 151.0 %copy-start.4 = (f32[1,88,32]{1,2,0:T(8,128)S(1)}, f32[1,88,32]{1,2,0:T(8,128)}, u32[]{:S(2)}) copy-start(f32[1,88,32]{1,2,0:T(8,128)} %param.22) | copy-start | bytes 33796
  0.7 151.0 %copy-start.5 = (f32[1,88,32]{1,2,0:T(8,128)S(1)}, f32[1,88,32]{1,2,0:T(8,128)}, u32[]{:S(2)}) copy-start(f32[1,88,32]{1,2,0:T(8,128)} %param.23) | copy-start | bytes 33796
  0.7 152.3 %copy-start = (f32[1,32,256]{2,1,0:T(8,128)S(1)}, f32[1,32,256]{2,1,0:T(8,128)}, u32[]{:S(2)}) copy-start(f32[1,32,256]{2,1,0:T(8,128)} %second_ref.1) | copy-start | bytes 98308
  0.7 152.3 %copy-start.2 = (f32[1,32,256]{2,1,0:T(8,128)S(1)}, f32[1,32,256]{2,1,0:T(8,128)}, u32[]{:S(2)}) copy-start(f32[1,32,256]{2,1,0:T(8,128)} %param.24) | copy-start | bytes 98308
  0.7 152.3 %copy-start.3 = (f32[1,32,256]{2,1,0:T(8,128)S(1)}, f32[1,32,256]{2,1,0:T(8,128)}, u32[]{:S(2)}) copy-start(f32[1,32,256]{2,1,0:T(8,128)} %param.25) | copy-start | bytes 98308
